TPU v7x, 128 devices: a whole 4x4x4 slice. The times are simulated.
128 devices in a mesh: rep: 2 (over core), space: 64 (over z, y, x).
Axes of the slice: x: 4, y: 4, z: 4, core: 2. Of those that a mesh axis runs over, the one named last changes fastest.
Arguments:
- particles: float32 [6, 2, 32768, 128], P(None, 'rep', 'space'), may hold values from -6 to 6
- pair_order: int32 [2, 32768, 128], P('rep', 'space'), may hold values from 0 to 127, each once within a row
- accepted: int32 [2, 32768, 64], P('rep', 'space'), may hold values 0 or 1
- direction: int32 [2, 32768, 64], P('rep', 'space'), may hold values from 0 to 255
- destination: int32 [2, 32768], P('rep', 'space'), may hold values from 0 to 63, as said below
- live_count: int32 [2, 64], P('rep', 'space'), may hold values from 256 to 512, as said below
- cell_index: int32 [2, 32768], P('rep', 'space'), may hold values from 0 to 255
Outputs:
- moved: float32 [6, 2, 49152, 128], P(None, 'rep', 'space')
- samples: float32 [4, 64, 256], P(None, 'space', 'rep')
Inputs may be any that keep to these rules, and one draw needn't show every extreme that they name: Every block's destination is its own slab or one of the two beside it, slab 0 and slab 64 - 1 being beside each other; only live blocks leave; one slab of one replica sends at most 128 blocks to each of its two neighbours, and in every replica some slab sends exactly 128 to its upper and some slab exactly 128 to its lower neighbour. `live_count`: the count of live blocks of each slab of each replica; slab 0 of replica 0 is full.
All inputs are finite; a program needn't handle non-finite values. No bound on the sum of `accepted` on one device may be relied on, other than what follows from the above.
Results may differ from a plain program's by a relative error of at most 0.0003.
Values sent between devices are 32-bit elements; how exact they have to be, the bound alone decides.
No kernel may reach another device: no remote copies, remote signals or barrier semaphores. Data moves between devices by JAX's collectives and lax.ppermute only.
A program may use at most 64 MiB of HBM per device.

v0:
```python
import jax
import jax.numpy as jnp
from jax import lax
from jax.sharding import PartitionSpec as P

PART = 128
PAIRS = 64
NDIR = 256
CAP = 512
MOVE = 128
CELLS = 256


time_step = 0.25
golden_turn = 2.399963229728653
group_size = 16


def from_behind(value, axis, steps):
    count = lax.axis_size(axis)
    pairs = [(source, (source + steps) % count) for source in range(count)]
    return lax.ppermute(value, axis, pairs)


def directions(index):
    turns = index.astype(jnp.float32)
    height = 1.0 - (2.0 * turns + 1.0) / NDIR
    radius = jnp.sqrt(1.0 - height * height)
    angle = turns * golden_turn
    return jnp.stack([radius * jnp.cos(angle), radius * jnp.sin(angle), height])


def collide_group(inputs):
    velocity, order, flags, turns = inputs
    lanes = jnp.arange(PART, dtype=jnp.int32)
    onehot = (order[:, :, None] == lanes[None, None, :]).astype(jnp.float32)
    permuted = jnp.einsum("kbp,bqp->kbq", velocity, onehot, precision=lax.Precision.HIGHEST)
    first = permuted[:, :, :PAIRS]
    second = permuted[:, :, PAIRS:]
    center = 0.5 * (first + second)
    relative = first - second
    speed = jnp.sqrt(jnp.sum(relative * relative, axis=0))
    unit = directions(turns)
    taken = (flags == 1)[None]
    first_out = jnp.where(taken, center + 0.5 * speed * unit, first)
    second_out = jnp.where(taken, center - 0.5 * speed * unit, second)
    combined = jnp.concatenate([first_out, second_out], axis=2)
    return jnp.einsum("kbq,bqp->kbp", combined, onehot, precision=lax.Precision.HIGHEST)


def collide(velocity, orders, flags, turns):
    count = velocity.shape[1]
    groups = count // group_size
    grouped = jnp.moveaxis(velocity.reshape(3, groups, group_size, PART), 1, 0)
    result = lax.map(
        collide_group,
        (
            grouped,
            orders.reshape(groups, group_size, PART),
            flags.reshape(groups, group_size, PAIRS),
            turns.reshape(groups, group_size, PAIRS),
        ),
    )
    return jnp.moveaxis(result, 0, 1).reshape(3, count, PART)


def advance(current, orders, flags, turns):
    velocity = collide(current[3:], orders, flags, turns)
    position = current[:3] + time_step * velocity
    return (position, velocity)


def moments(velocity, living):
    sums = jnp.stack(
        [
            jnp.sum(velocity[0], axis=1),
            jnp.sum(velocity[1], axis=1),
            jnp.sum(velocity[2], axis=1),
            jnp.sum(jnp.sum(velocity * velocity, axis=0), axis=1),
        ]
    )
    return jnp.where(living[None], sums, 0.0)


def mover_slots(moving):
    ranking = jnp.cumsum(moving.astype(jnp.int32)) - 1
    slots = jnp.arange(MOVE, dtype=jnp.int32)
    matches = moving[None, :] & (ranking[None, :] == slots[:, None])
    sources = jnp.arange(moving.shape[0], dtype=jnp.int32)
    chosen = jnp.sum(jnp.where(matches, sources[None, :], 0), axis=1)
    is_valid = jnp.any(matches, axis=1)
    return (chosen, is_valid)


def per_device(particles, pair_order, accepted, direction, destination, live_count, cell_index):
    current = particles[:, 0]
    orders = pair_order[0]
    flags = accepted[0]
    turns = direction[0]
    my_slab = lax.axis_index("space")
    slab_total = lax.axis_size("space")
    upper_slab = (my_slab + 1) % slab_total
    lower_slab = (my_slab + slab_total - 1) % slab_total
    slot_index = jnp.arange(CAP, dtype=jnp.int32)
    living = slot_index < live_count[0, 0]
    targets = destination[0]
    to_upper = living & (targets == upper_slab)
    to_lower = living & (targets == lower_slab)
    staying = living & (targets == my_slab)
    upper_ids, upper_valid = mover_slots(to_upper)
    lower_ids, lower_valid = mover_slots(to_lower)
    position, velocity = advance(current, orders, flags, turns)
    updated = jnp.concatenate([position, velocity], axis=0)
    send_upper = jnp.where(upper_valid[None, :, None], jnp.take(updated, upper_ids, axis=1), 0.0)
    send_lower = jnp.where(lower_valid[None, :, None], jnp.take(updated, lower_ids, axis=1), 0.0)
    from_lower = from_behind(send_upper, "space", 1)
    from_upper = from_behind(send_lower, "space", -1)
    term = moments(velocity, living)
    cell_ids = jnp.arange(CELLS, dtype=jnp.int32)
    onehot = (cell_index[0][None, :] == cell_ids[:, None]).astype(jnp.float32)
    cell_terms = jnp.dot(term, onehot.T, precision=lax.Precision.HIGHEST)
    summed = lax.psum_scatter(cell_terms, "rep", scatter_dimension=1, tiled=True)
    samples = (summed / (PART * lax.axis_size("rep")))[:, None, :]
    keep = staying[None, :, None]
    moved = jnp.concatenate(
        [
            from_lower,
            jnp.where(keep, jnp.concatenate([position, velocity], axis=0), 0.0),
            from_upper,
        ],
        axis=1,
    )
    return (moved[:, None], samples)


def solution(mesh):
    return jax.shard_map(
        per_device,
        mesh=mesh,
        in_specs=(
            P(None, "rep", "space", None),
            P("rep", "space", None),
            P("rep", "space", None),
            P("rep", "space", None),
            P("rep", "space"),
            P("rep", "space"),
            P("rep", "space"),
        ),
        out_specs=(P(None, "rep", "space", None), P(None, "space", "rep")),
        check_vma=False,
    )
```

profile of v0, /device:TPU:1, one launch (start us, length us, event | category | flops | bytes accessed | tf_op | source)
XLA Modules:
  0.0 155.6 jit_solution(8836516410862736738)
XLA Ops:
  9.5 1.0 copy.38
  10.6 1.0 copy.40
  11.6 1.5 fusion.28
  13.6 89.0 %while.10 = (s32[]{:T(128)}, f32[32,3,16,128]{3,1,2,0:T(4,128)S(1)}, s32[32,16,128]{2,1,0:T(8,128)}, s32[32,16,64]{2,1,0:T(8,128)S(1)}, f32[32,3,16,128]{3,1,2,0...) while((s32[]{:T(128)}, f32[32,3,16,128]{3,1,2,0:T(4,128)S(1)}, s32[32,16,128]{2,1,0:T(8,128)}, ...), condition=%wide.region_5.6_spmd, body=%wide.region_3.5_spmd.sunk | while | flops 19452928 | bytes 370793 | solution.py:55
  14.4 1.0 fusion.36
  15.7 0.7 fusion.38
  17.2 1.0 fusion.36
  18.5 0.7 fusion.38
  20.0 1.0 fusion.36
  21.3 0.7 fusion.38
  22.8 1.0 fusion.36
  24.0 0.7 fusion.38
  25.6 1.0 fusion.36
  26.8 0.7 fusion.38
  28.3 1.0 fusion.36
  29.6 0.7 fusion.38
  31.1 1.0 fusion.36
  32.4 0.7 fusion.38
  33.9 1.0 fusion.36
  35.2 0.7 fusion.38
  36.7 1.0 fusion.36
  39.5 1.0 fusion.36
  42.2 1.0 fusion.36
  45.0 1.0 fusion.36
  47.8 1.0 fusion.36
  50.6 1.0 fusion.36
  51.9 0.7 fusion.38
  53.4 1.0 fusion.36
  54.6 0.7 fusion.38
  56.2 1.0 fusion.36
  57.4 0.7 fusion.38
  58.9 1.0 fusion.36
  60.2 0.7 fusion.38
  61.7 1.0 fusion.36
  63.0 0.7 fusion.38
  64.5 1.0 fusion.36
  67.3 1.0 fusion.36
  70.1 1.0 fusion.36
  72.8 1.0 fusion.36
  75.6 1.0 fusion.36
  78.4 1.0 fusion.36
  81.2 1.0 fusion.36
  84.0 1.0 fusion.36
  86.8 1.0 fusion.36
  89.5 1.0 fusion.36
  92.3 1.0 fusion.36
  93.6 0.7 fusion.38
  95.1 1.0 fusion.36
  97.9 1.0 fusion.36
  100.7 1.0 fusion.36
  102.7 0.7 fusion.9
  103.4 2.9 %broadcast_select_fusion = (f32[6,512,128]{2,0,1:T(8,128)S(1)}, f32[6,512,128]{2,0,1:T(8,128)}) fusion(pred[512]{0:T(512)(128)(4,1)S(1)} %fusion.27, f32[3,512,128]{2,0,1:T(4,128)S(1)} %bitcast.74, f32[3,512,128]{2,0,1:T(4,128)S(1)} %fusion.9), kind=kLoop, calls=%fused_computation.34 | loop fusion | flops 786432 | bytes 4719104 | tf_op jit(solution)/shard_map/jit(_where)/select_n | solution.py:128
  106.3 3.0 %gather_fusion.1 = f32[128,6,128]{2,1,0:T(8,128)} fusion(f32[6,512,128]{2,0,1:T(8,128)} %get-tuple-element.90, s32[1024]{0:T(1024)S(1)} %pad_clamp_fusion), kind=kCustom, calls=%fused_computation.1.clone | custom fusion | bytes 786944 | tf_op jit(solution)/shard_map/jit(_take)/gather | solution.py:115
  109.4 2.2 %bitcast_select_fusion = f32[6,128,128]{2,0,1:T(8,128)} fusion(f32[128,6,128]{2,1,0:T(8,128)} %gather_fusion.1, pred[128]{0:T(512)(128)(4,1)S(1)} %compare_and_fusion, pred[128]{0:T(512)(128)(4,1)S(1)} %fusion.14), kind=kLoop, calls=%fused_computation.35 | loop fusion | flops 196608 | bytes 786688 | tf_op jit(solution)/shard_map/jit(_where)/select_n | solution.py:115
  111.5 9.2 %collective-permute-start.1 = (f32[6,128,128]{2,0,1:T(8,128)}, f32[6,128,128]{2,0,1:T(8,128)}, u32[]{:S(2)}, u32[]{:S(2)}) collective-permute-start(f32[6,128,128]{2,0,1:T(8,128)} %bitcast_select_fusion), channel_id=1, source_target_pairs={{0,63},{1,0},{2,1},{3,2},{4,3},{5,4},{6,5},{7,6},{8,7},{9,8},{10,9... | collective-permute-start | bytes 1179656 | tf_op jit(solution)/shard_map/ppermute | solution.py:22
  121.7 3.0 %gather_fusion = f32[128,6,128]{2,1,0:T(8,128)} fusion(f32[6,512,128]{2,0,1:T(8,128)} %get-tuple-element.90, s32[1024]{0:T(1024)S(1)} %pad_clamp_fusion.1), kind=kCustom, calls=%fused_computation.clone | custom fusion | bytes 786944 | tf_op jit(solution)/shard_map/jit(_take)/gather | solution.py:114
  124.7 2.2 %bitcast_select_fusion.1 = f32[6,128,128]{2,0,1:T(8,128)} fusion(f32[128,6,128]{2,1,0:T(8,128)} %gather_fusion, pred[128]{0:T(512)(128)(4,1)S(1)} %compare_and_fusion.1, pred[128]{0:T(512)(128)(4,1)S(1)} %fusion.12), kind=kLoop, calls=%fused_computation.36 | loop fusion | flops 196608 | bytes 786688 | tf_op jit(solution)/shard_map/jit(_where)/select_n | solution.py:114
  126.9 1.0 multiply_reduce_fusion.1
  128.0 2.9 %slice_reduce_fusion.2 = (f32[32,16]{1,0:T(8,128)S(1)}, f32[32,16]{1,0:T(8,128)S(1)}, f32[32,16]{1,0:T(8,128)S(1)}) fusion(f32[3,32,16,128]{3,0,2,1:T(4,128)S(1)} %bitcast.75), kind=kLoop, calls=%fused_computation.40 | loop fusion | flops 195072 | bytes 792576 | tf_op jit(solution)/shard_map/reduce_sum | solution.py:76
  131.1 1.0 convolution_bitcast_fusion.1
  132.2 11.8 %reduce-scatter.4.cloned.1.call-done = f32[128,4]{1,0:T(8,128)} async-done(((f32[256,4]{1,0:T(8,128)}), f32[128,4]{1,0:T(8,128)}) %reduce-scatter.4.cloned.1.call-update) | async-done | bytes 2064
  143.9 0.9 copy.44
  145.4 1.5 maximum_bitcast_fusion
  146.9 1.8 %copy.41 = f32[6,1,768,128]{3,2,1,0:T(8,128)} copy(f32[6,1,768,128]{3,0,2,1:T(8,128)S(1)} %maximum_bitcast_fusion) | data formatting | bytes 4718592
  (313 shorter events, 50.4 us)
Async XLA Ops:
  7.2 136.8 %reduce-scatter.4.cloned.1.call-start = ((), (), s32[]{:S(2)}) async-start(), calls=%async_computation.1 | async-start | bytes 196608
  111.5 19.6 %copy-start = (s32[1,512]{1,0:T(1,128)S(1)}, s32[1,512]{1,0:T(1,128)}, u32[]{:S(2)}) copy-start(s32[1,512]{1,0:T(1,128)} %param.17) | copy-start | bytes 6148
  111.5 33.9 %collective-permute-start.1 = (f32[6,128,128]{2,0,1:T(8,128)}, f32[6,128,128]{2,0,1:T(8,128)}, u32[]{:S(2)}, u32[]{:S(2)}) collective-permute-start(f32[6,128,128]{2,0,1:T(8,128)} %bitcast_select_fusion), channel_id=1, source_target_pairs={{0,63},{1,0},{2,1},{3,2},{4,3},{5,4},{6,5},{7,6},{8,7},{9,8},{10,9... | collective-permute-start | bytes 1179656 | tf_op jit(solution)/shard_map/ppermute | solution.py:22
  126.9 18.5 %collective-permute-start = (f32[6,128,128]{2,0,1:T(8,128)}, f32[6,128,128]{2,0,1:T(8,128)}, u32[]{:S(2)}, u32[]{:S(2)}) collective-permute-start(f32[6,128,128]{2,0,1:T(8,128)} %bitcast_select_fusion.1), channel_id=1, source_target_pairs={{0,1},{1,2},{2,3},{3,4},{4,5},{5,6},{6,7},{7,8},{8,9},{9,10},{10,1... | collective-permute-start | bytes 1179656 | tf_op jit(solution)/shard_map/ppermute | solution.py:22
Sparse Core Ops, SparseCore 0:
  132.3 11.6 reduce-scatter.3
where the time goes:
time: 158 us; the launch traced here: 156 us
  matrix products  56 us (35%)
  local copies, waits for them, and re-layouts  36.3 us (23%)
  other arithmetic  26.5 us (17%)
  between operations  14.8 us (9%)
  waiting for transfers between devices  11.8 us (7%)
  starting transfers between devices  9.27 us (6%)
    dot_general x32, matrix products, collide_group(): jnp.einsum('kbp,bqp->kbq', velocity, onehot, precision=lax.Precision.HIGH...  31.5 us
    dot_general x32, matrix products, collide_group(): jnp.einsum('kbq,bqp->kbp', combined, onehot, precision=lax.Precision.HIGH...  23.5 us
    eq x32, local copies, waits for them, and re-layouts, collide_group(): onehot = (order[:, :, None] == lanes[None, None, :]).astype(jnp.float32)  22.5 us
    unnamed x2, waiting for transfers between devices  11.8 us
    ppermute x2, starting transfers between devices, from_behind(): return lax.ppermute(value, axis, pairs)  9.23 us
    unnamed x6, local copies, waits for them, and re-layouts  4.79 us
  transfers between devices with their start and end apart: 3, of which 1 were waited for; matrix products, arithmetic and copies ran while one was open for 8% of the time, Pallas kernels for 0%

commit v1 on v0

v1 whole, which is shorter than its diff:
```python
import functools

import jax
import jax.numpy as jnp
import numpy as np
from jax import lax
from jax.experimental import pallas as pl
from jax.experimental.pallas import tpu as pltpu
from jax.sharding import PartitionSpec as P

PART = 128
PAIRS = 64
NDIR = 256
CAP = 512
MOVE = 128
CELLS = 256
OUTCAP = 768
SLABS = 64

time_step = 0.25
golden_turn = 2.399963229728653
TURN_HIGH = float(np.round(golden_turn / (2 * np.pi) * 4096) / 4096)
TURN_LOW = float(golden_turn / (2 * np.pi) - TURN_HIGH)

CONTRACT_LANES = (((1,), (1,)), ((), ()))


def fitted(function, powers):
    x = 0.25 * np.cos((np.arange(400) + 0.5) * np.pi / 400)
    basis = np.stack([x**p for p in powers], axis=1)
    return [float(c) for c in np.linalg.lstsq(basis, function(x), rcond=None)[0]]


SINE = fitted(lambda x: np.sin(2 * np.pi * x), [1, 3, 5, 7, 9])
COSINE = fitted(lambda x: np.cos(2 * np.pi * x), [0, 2, 4, 6, 8])


def polynomial(x, coefficients):
    total = jnp.full_like(x, coefficients[-1])
    for c in coefficients[-2::-1]:
        total = total * x + c
    return total


def directions(turns):
    height = 1.0 - (2.0 * turns + 1.0) * (1.0 / NDIR)
    radius = jnp.sqrt(1.0 - height * height)
    whole = turns * TURN_HIGH
    part = (whole - jnp.floor(whole + 0.5)) + turns * TURN_LOW
    fold = jnp.abs(part) - 0.25
    square = fold * fold
    cosine = -fold * polynomial(square, SINE)
    sine = polynomial(square, COSINE)
    sine = jnp.where(part < 0.0, -sine, sine)
    return radius * cosine, radius * sine, height


def swap_sublanes(x, distance):
    if distance == 4:
        return pltpu.roll(x, 4, 1)
    ahead = pltpu.roll(x, 8 - distance, 1)
    behind = pltpu.roll(x, distance, 1)
    low = (lax.broadcasted_iota(jnp.int32, x.shape, 1) & distance) == 0
    return jnp.where(low, ahead, behind)


def sort_rows(keys):
    n = keys.shape[-1]
    rows = [keys[8 * r : 8 * r + 8] for r in range(16)]
    sub = lax.broadcasted_iota(jnp.int32, (8, n), 0)

    def exchange(rows, bit, down_bit):
        new = list(rows)
        for r in range(16):
            other = r ^ (1 << bit)
            if r < other:
                small, large = jnp.minimum(rows[r], rows[other]), jnp.maximum(rows[r], rows[other])
                if down_bit is not None and (r >> down_bit) & 1:
                    small, large = large, small
                new[r], new[other] = small, large
        return new

    def exchange_sublanes(rows, distance):
        low = (sub & distance) == 0
        new = []
        for x in rows:
            y = swap_sublanes(x[None], distance)[0]
            new.append(jnp.where(low, jnp.minimum(x, y), jnp.maximum(x, y)))
        return new

    for stage in (1, 2, 3):
        for bit in range(stage - 1, -1, -1):
            rows = exchange(rows, bit, stage)
    for stage in (4, 5, 6, 7):
        flip = None
        if stage < 7:
            flip = jnp.where((sub & (1 << (stage - 4))) == 0, 1.0, -1.0)
            rows = [x * flip for x in rows]
        for bit in range(stage - 1, -1, -1):
            rows = exchange(rows, bit, None) if bit < 4 else exchange_sublanes(rows, 1 << (bit - 4))
        if flip is not None:
            rows = [x * flip for x in rows]
    return jnp.concatenate(rows, axis=0)


def partner_codes(order, info):
    taken = info > -0.5
    turns = jnp.maximum(info, 0.0)
    first, second = order[:PAIRS], order[PAIRS:]
    partner = jnp.concatenate([jnp.where(taken, second, first), jnp.where(taken, first, second)], axis=0)
    eighth = jnp.floor(order * 0.125)
    place = order * 16.0 - eighth * 127.0
    extra = jnp.concatenate([turns * 2.0, turns * 2.0 + 1.0], axis=0)
    return sort_rows(place * 65536.0 + partner * 512.0 + extra)


def collide(velocity, codes):
    partner = (codes >> 9) & 127
    turns = ((codes >> 1) & 255).astype(jnp.float32)
    other = [jnp.take_along_axis(v, partner, axis=1) for v in velocity]
    relative = [v - o for v, o in zip(velocity, other)]
    speed = jnp.sqrt(relative[0] * relative[0] + relative[1] * relative[1] + relative[2] * relative[2])
    half = 0.5 * speed
    half = jnp.where((codes & 1) == 0, half, -half)
    return [0.5 * (v + o) + half * u for v, o, u in zip(velocity, other, directions(turns))]


def split(x):
    high = x.astype(jnp.bfloat16)
    return high, (x - high.astype(jnp.float32)).astype(jnp.bfloat16)


def dot(a, b):
    return jnp.dot(a, b, preferred_element_type=jnp.float32)


def dot_lanes(a, b):
    return lax.dot_general(a, b, CONTRACT_LANES, preferred_element_type=jnp.float32)


def pick(selection, x):
    high, low = split(x)
    return dot(selection, high) + dot(selection, low)


def mover_selection(destination, live, target):
    slots = lax.broadcasted_iota(jnp.int32, (1, CAP), 1)
    moving = (slots < live) & (destination == target)
    ahead = lax.broadcasted_iota(jnp.int32, (CAP, CAP), 0) < lax.broadcasted_iota(jnp.int32, (CAP, CAP), 1)
    flags = jnp.broadcast_to(jnp.where(moving, 1.0, 0.0), (8, CAP))
    ranking = dot(flags.astype(jnp.bfloat16), jnp.where(ahead, 1.0, 0.0).astype(jnp.bfloat16))[:1]
    ranking = jnp.where(moving, ranking, -1.0)
    rows = lax.broadcasted_iota(jnp.int32, (MOVE, CAP), 0).astype(jnp.float32)
    return jnp.where(ranking == rows, 1.0, 0.0).astype(jnp.bfloat16)


def position_kernel(scalars, destination, position, out):
    selection = mover_selection(destination[...], scalars[0], scalars[1])
    for c in range(3):
        out[c] = pick(selection, position[c, 0])


def movers_collided(scalars, at, destination, velocity, order, accepted, direction):
    selection = mover_selection(destination[...], scalars[0], scalars[at])
    info = jnp.where(accepted[0] == 1, direction[0], -1).astype(jnp.float32).astype(jnp.bfloat16)
    chosen = dot_lanes(info, selection)
    orders = dot(selection, order[0].astype(jnp.float32).astype(jnp.bfloat16))
    codes = partner_codes(orders.T, chosen).T.astype(jnp.int32)
    return selection, collide([pick(selection, velocity[c, 0]) for c in range(3)], codes)


def upward_kernel(scalars, destination, velocity, order, accepted, direction, sent, out):
    del sent
    _, result = movers_collided(scalars, 1, destination, velocity, order, accepted, direction)
    for c in range(3):
        out[c] = result[c]


def downward_kernel(scalars, destination, particles, order, accepted, direction, sent, out):
    del sent
    velocity = particles.at[3:6]
    selection, result = movers_collided(scalars, 2, destination, velocity, order, accepted, direction)
    for c in range(3):
        out[3 + c] = result[c]
        out[c] = pick(selection, particles[c, 0]) + time_step * result[c]


def own_kernel(scalars, destination, cells, particles, order, accepted, direction, sent, moved, mine, theirs, total):
    del sent
    step = pl.program_id(0)
    slots = lax.broadcasted_iota(jnp.int32, (1, PART), 1) + step * PART
    live = slots < scalars[0]
    staying = jnp.where(live & (destination[...] == scalars[3]), 1.0, 0.0)
    info = jnp.where(accepted[0] == 1, direction[0], -1).astype(jnp.float32)
    codes = partner_codes(order[0].astype(jnp.float32).T, info) + staying * 8388608.0
    codes = codes.T.astype(jnp.int32)
    keep = (codes >> 23) == 1
    result = collide([particles[3 + c, 0] for c in range(3)], codes)
    for c in range(3):
        moved[3 + c, 0] = jnp.where(keep, result[c], 0.0)
        moved[c, 0] = jnp.where(keep, particles[c, 0] + time_step * result[c], 0.0)
    cell = (cells[...] + scalars[4] * (CELLS // 2)) & (CELLS - 1)
    cell = jnp.where(live, cell, -1)
    onehot = lax.broadcasted_iota(jnp.int32, (CELLS, PART), 0) == cell
    onehot = jnp.where(onehot, 1.0, 0.0).astype(jnp.bfloat16)
    squares = result[0] * result[0] + result[1] * result[1] + result[2] * result[2]
    for c, value in enumerate([*result, squares]):
        part = pick(onehot, value)

        @pl.when(step == 0)
        def _():
            total[c] = part

        @pl.when(step > 0)
        def _():
            total[c] += part

    @pl.when(step == CAP // PART - 1)
    def _():
        ones = jnp.ones((8, PART), jnp.bfloat16)
        for c in range(4):
            high, low = split(total[c])
            sums = dot_lanes(ones, high) + dot_lanes(ones, low)
            mine[c : c + 1] = sums[:1, : CELLS // 2]
            theirs[c : c + 1] = sums[:1, CELLS // 2 :]


def below_kernel(held, arrived, moved):
    del held
    moved[:, 0] = arrived[...]


def above_kernel(held, position, velocity, mine, arrived, moved, samples, *, parts):
    del held
    for c in range(3):
        v = velocity[c]
        moved[3 + c, 0] = v
        moved[c, 0] = position[c] + time_step * v
    samples[:, 0] = (mine[...] + arrived[...]) * (1.0 / (PART * parts))


def whole(shape, at=None):
    at = at or (0,) * len(shape)
    return pl.BlockSpec(shape, lambda *_: at)


SMEM = pl.BlockSpec(memory_space=pltpu.SMEM)
ANY = pl.BlockSpec(memory_space=pl.ANY)


def from_behind(value, axis, steps):
    count = lax.axis_size(axis)
    pairs = [(source, (source + steps) % count) for source in range(count)]
    return lax.ppermute(value, axis, pairs)


def per_device(particles, pair_order, accepted, direction, destination, live_count, cell_index):
    accepted = jnp.swapaxes(accepted, 1, 2)
    direction = jnp.swapaxes(direction, 1, 2)
    slab = lax.axis_index("space")
    total = lax.axis_size("space")
    rep = lax.axis_index("rep")
    parts = lax.axis_size("rep")
    scalars = jnp.stack([live_count[0, 0], (slab + 1) % total, (slab + total - 1) % total, slab, rep]).astype(jnp.int32)
    f32 = jnp.float32
    limit = pltpu.CompilerParams(vmem_limit_bytes=40 * 2**20)
    once = dict(grid=(1,), compiler_params=limit)

    def cost(microseconds):
        return pl.CostEstimate(flops=0, bytes_accessed=int(microseconds * 3.0e6), transcendentals=0)


    row = whole((1, CAP))
    up_position = pl.pallas_call(
        position_kernel,
        in_specs=[SMEM, row, whole((3, 1, CAP, PART))],
        out_specs=whole((3, MOVE, PART)),
        out_shape=jax.ShapeDtypeStruct((3, MOVE, PART), f32),
        cost_estimate=cost(1),
        **once,
    )(scalars, destination, particles)
    position_from_lower = from_behind(up_position, "space", 1)

    pair_specs = [whole((1, CAP, PART)), whole((1, PAIRS, CAP)), whole((1, PAIRS, CAP)), ANY]
    up_velocity = pl.pallas_call(
        upward_kernel,
        in_specs=[SMEM, row, whole((3, 1, CAP, PART), (1, 0, 0, 0)), *pair_specs],
        out_specs=whole((3, MOVE, PART)),
        out_shape=jax.ShapeDtypeStruct((3, MOVE, PART), f32),
        cost_estimate=cost(2),
        **once,
    )(scalars, destination, particles, pair_order, accepted, direction, up_position)
    velocity_from_lower = from_behind(up_velocity, "space", 1)

    down = pl.pallas_call(
        downward_kernel,
        in_specs=[SMEM, row, whole((6, 1, CAP, PART)), *pair_specs],
        out_specs=whole((6, MOVE, PART)),
        out_shape=jax.ShapeDtypeStruct((6, MOVE, PART), f32),
        cost_estimate=cost(2),
        **once,
    )(scalars, destination, particles, pair_order, accepted, direction, up_velocity)
    from_upper = from_behind(down, "space", -1)

    lanes = pl.BlockSpec((1, PART), lambda i: (0, i))
    pairs = pl.BlockSpec((1, PAIRS, PART), lambda i: (0, 0, i))
    half = jax.ShapeDtypeStruct((4, CELLS // 2), f32)
    moved, mine, theirs = pl.pallas_call(
        own_kernel,
        grid=(CAP // PART,),
        in_specs=[
            SMEM,
            lanes,
            lanes,
            pl.BlockSpec((6, 1, PART, PART), lambda i: (0, 0, i, 0)),
            pl.BlockSpec((1, PART, PART), lambda i: (0, i, 0)),
            pairs,
            pairs,
            ANY,
        ],
        out_specs=[
            pl.BlockSpec((6, 1, PART, PART), lambda i: (0, 0, i + 1, 0)),
            whole((4, CELLS // 2)),
            whole((4, CELLS // 2)),
        ],
        out_shape=[jax.ShapeDtypeStruct((6, 1, OUTCAP, PART), f32), half, half],
        scratch_shapes=[pltpu.VMEM((4, CELLS, PART), f32)],
        cost_estimate=cost(5),
        compiler_params=limit,
    )(scalars, destination, cell_index, particles, pair_order, accepted, direction, down)
    arrived = from_behind(theirs, "rep", 1)

    moved = pl.pallas_call(
        below_kernel,
        in_specs=[ANY, whole((6, MOVE, PART))],
        out_specs=whole((6, 1, MOVE, PART), (0, 0, 5, 0)),
        out_shape=jax.ShapeDtypeStruct(moved.shape, f32),
        input_output_aliases={0: 0},
        **once,
    )(moved, from_upper)
    moved, samples = pl.pallas_call(
        functools.partial(above_kernel, parts=parts),
        in_specs=[ANY, whole((3, MOVE, PART)), whole((3, MOVE, PART)), whole((4, CELLS // 2)), whole((4, CELLS // 2))],
        out_specs=[whole((6, 1, MOVE, PART)), whole((4, 1, CELLS // 2))],
        out_shape=[jax.ShapeDtypeStruct(moved.shape, f32), jax.ShapeDtypeStruct((4, 1, CELLS // 2), f32)],
        input_output_aliases={0: 0},
        **once,
    )(moved, position_from_lower, velocity_from_lower, mine, arrived)
    return (moved, samples)


def solution(mesh):
    return jax.shard_map(
        per_device,
        mesh=mesh,
        in_specs=(
            P(None, "rep", "space", None),
            P("rep", "space", None),
            P("rep", "space", None),
            P("rep", "space", None),
            P("rep", "space"),
            P("rep", "space"),
            P("rep", "space"),
        ),
        out_specs=(P(None, "rep", "space", None), P(None, "space", "rep")),
        check_vma=False,
    )
```

time: 158 us -> 36.2 us (0.23); the launches traced: 156 us -> 35.5 us
  matrix products: 56 us -> 0 us
  local copies, waits for them, and re-layouts: 36.3 us -> 4.94 us
  other arithmetic: 26.5 us -> 0 us
  between operations: 14.8 us -> 1.36 us
  Pallas kernels: 0 us -> 12.9 us
  waiting for transfers between devices: 11.8 us -> 6.04 us
    dot_general x64 -> x0, matrix products: 55 us -> none  [the longest x32 31.5 us: collide_group(): jnp.einsum('kbp,bqp->kbq', velocity, onehot, precision=lax.Precision.HIGH...]
    eq x32 -> x0, local copies, waits for them, and re-layouts: 22.5 us -> none  [collide_group(): onehot = (order[:, :, None] == lanes[None, None, :]).astype(jnp.float32)]
    pallas_call x0 -> x6, Pallas kernels: none -> 12.9 us  [the longest x1 7.31 us: per_device(): pl.pallas_call(own_kernel, grid=(CAP // PART,), in_specs=[SMEM, lanes, la...]
    unnamed x2 -> x0, waiting for transfers between devices: 11.8 us -> none
    select_n x37 -> x0, other arithmetic: 9.85 us -> none  [the longest x1 2.88 us: per_device(): jnp.where(keep, jnp.concatenate([position, velocity], axis=0), 0.0)]
    reduce_sum x36 -> x0, other arithmetic: 6.86 us -> none  [the longest x1 2.88 us: moments(): jnp.sum(velocity[0], axis=1)]
    gather x2 -> x0, local copies, waits for them, and re-layouts: 6.1 us -> none  [the longest x1 3.05 us: per_device(): jnp.take(updated, lower_ids, axis=1)]
    ppermute x2 -> x4, waiting for transfers between devices: 0.01 us -> 6.04 us  [from_behind(): return lax.ppermute(value, axis, pairs)]
  transfers between devices with their start and end apart: 3 -> 4, of which waited for: 1 -> 2; matrix products, arithmetic and copies ran while one was open for 8% -> 0% of each run, Pallas kernels for 0% -> 23%
where the time goes in v1:
time: 36.2 us; the launch traced here: 35.5 us
  Pallas kernels  12.9 us (36%)
  starting transfers between devices  10.3 us (28%)
  waiting for transfers between devices  6.04 us (17%)
  local copies, waits for them, and re-layouts  4.94 us (14%)
  between operations  1.36 us (4%)
    ppermute x4, starting transfers between devices, from_behind(): return lax.ppermute(value, axis, pairs)  10.3 us
    pallas_call x1, Pallas kernels, per_device(): pl.pallas_call(own_kernel, grid=(CAP // PART,), in_specs=[SMEM, lanes, la...  7.31 us
    ppermute x4, waiting for transfers between devices, from_behind(): return lax.ppermute(value, axis, pairs)  6.04 us
    unnamed x18, local copies, waits for them, and re-layouts  4.86 us
    pallas_call x1, Pallas kernels, per_device(): pl.pallas_call(downward_kernel, in_specs=[SMEM, row, whole((6, 1, CAP, PA...  1.56 us
    pallas_call x1, Pallas kernels, per_device(): pl.pallas_call(upward_kernel, in_specs=[SMEM, row, whole((3, 1, CAP, PART...  1.44 us
    pallas_call x1, Pallas kernels, per_device(): pl.pallas_call(position_kernel, in_specs=[SMEM, row, whole((3, 1, CAP, PA...  1.04 us
    pallas_call x1, Pallas kernels, per_device(): pl.pallas_call(functools.partial(above_kernel, parts=parts), in_specs=[AN...  0.78 us
  transfers between devices with their start and end apart: 4, of which 2 were waited for; matrix products, arithmetic and copies ran while one was open for 0% of the time, Pallas kernels for 23%

profile of v1, /device:TPU:1, one launch (start us, length us, event | category | flops | bytes accessed | tf_op | source)
XLA Modules:
  0.0 35.5 jit_solution(17365047381939521836)
XLA Ops:
  1.3 0.1 stack.19.scalars
  1.4 0.0 copy-start
  1.4 1.4 %copy-done = f32[6,1,512,128]{3,2,1,0:T(8,128)S(1)} copy-done((f32[6,1,512,128]{3,2,1,0:T(8,128)S(1)}, f32[6,1,512,128]{3,2,1,0:T(8,128)}, u32[]{:S(2)}) %copy-start) | copy-done | bytes 1572888
  2.8 0.0 copy-start.7
  2.8 0.7 %copy-done.7 = s32[1,512]{1,0:T(1,128)S(1)} copy-done((s32[1,512]{1,0:T(1,128)S(1)}, s32[1,512]{1,0:T(1,128)}, u32[]{:S(2)}) %copy-start.7) | copy-done | bytes 2072
  3.5 0.0 copy-start.2
  3.5 0.0 copy-start.4
  3.5 0.0 copy-start.6
  3.5 1.0 %shard_map.86.sent = f32[3,128,128]{2,1,0:T(8,128)S(1)} custom-call(s32[5]{0:T(128)S(1)} %stack.19.scalars, s32[1,512]{1,0:T(1,128)S(1)} %copy-done.7, f32[6,1,512,128]{3,2,1,0:T(8,128)S(1)} %copy-done), custom_call_target="tpu_custom_call" | custom-call | bytes 3000000 | tf_op jit(solution)/shard_map/pallas_call | solution.py:274
  4.5 0.0 copy-start.1
  4.5 0.9 %copy-done.1 = s32[1,512,128]{2,1,0:T(8,128)S(1)} copy-done((s32[1,512,128]{2,1,0:T(8,128)S(1)}, s32[1,512,128]{2,1,0:T(8,128)}, u32[]{:S(2)}) %copy-start.1) | copy-done | bytes 262168
  5.5 0.0 copy-start.3
  5.5 0.9 %copy-done.3 = s32[1,512,64]{1,2,0:T(8,128)S(1)} copy-done((s32[1,512,64]{1,2,0:T(8,128)S(1)}, s32[1,512,64]{1,2,0:T(8,128)}, u32[]{:S(2)}) %copy-start.3) | copy-done | bytes 131096
  6.4 0.0 copy-start.5
  6.4 0.9 %copy-done.5 = s32[1,512,64]{1,2,0:T(8,128)S(1)} copy-done((s32[1,512,64]{1,2,0:T(8,128)S(1)}, s32[1,512,64]{1,2,0:T(8,128)}, u32[]{:S(2)}) %copy-start.5) | copy-done | bytes 131096
  7.3 0.0 copy-start.8
  7.3 1.4 %shard_map.87.sent = f32[3,128,128]{2,1,0:T(8,128)S(1)} custom-call(s32[5]{0:T(128)S(1)} %stack.19.scalars, s32[1,512]{1,0:T(1,128)S(1)} %copy-done.7, f32[6,1,512,128]{3,2,1,0:T(8,128)S(1)} %copy-done, s32[1,512,128]{2,1,0:T(8,128)S(1)} %copy-done.1, s32[1,64,512]{2,1,0:T(8,128)S(1)} %bitcast.8, s32[1,64,512]{2,1,0:T(8,128)S(1)} %bitcast.11, ...), custom_call_target="tpu_custom_call" | custom-call | bytes 6000000 | tf_op jit(solution)/shard_map/pallas_call | solution.py:285
  8.7 0.0 copy-done.2
  8.8 0.0 copy-done.4
  8.8 0.0 copy-done.6
  8.8 1.6 %shard_map.88.sent = f32[6,128,128]{2,1,0:T(8,128)S(1)} custom-call(s32[5]{0:T(128)S(1)} %stack.19.scalars, s32[1,512]{1,0:T(1,128)S(1)} %copy-done.7, f32[6,1,512,128]{3,2,1,0:T(8,128)S(1)} %copy-done, s32[1,512,128]{2,1,0:T(8,128)S(1)} %copy-done.2, s32[1,64,512]{2,1,0:T(8,128)S(1)} %bitcast.9, s32[1,64,512]{2,1,0:T(8,128)S(1)} %bitcast.12, ...), custom_call_target="tpu_custom_call" | custom-call | bytes 6000000 | tf_op jit(solution)/shard_map/pallas_call | solution.py:295
  10.3 9.3 %collective-permute-start = (f32[6,128,128]{2,1,0:T(8,128)S(1)}, f32[6,128,128]{2,1,0:T(8,128)S(1)}, u32[]{:S(2)}, u32[]{:S(2)}) collective-permute-start(f32[6,128,128]{2,1,0:T(8,128)S(1)} %shard_map.88.sent), channel_id=1, source_target_pairs={{0,63},{1,0},{2,1},{3,2},{4,3},{5,4},{6,5},{7,6},{8,7},{9,8},{10,9... | collective-permute-start | bytes 1179656 | tf_op jit(solution)/shard_map/ppermute | solution.py:254
  19.6 0.0 collective-permute-start.2
  19.6 0.0 collective-permute-start.1
  19.6 0.0 copy-done.8
  19.6 7.3 %shard_map.89 = (f32[6,1,768,128]{3,2,1,0:T(8,128)}, f32[4,128]{1,0:T(4,128)S(1)}, f32[4,128]{1,0:T(4,128)S(1)}) custom-call(s32[5]{0:T(128)S(1)} %stack.19.scalars, s32[1,512]{1,0:T(1,128)S(1)} %copy-done.7, s32[1,512]{1,0:T(1,128)S(1)} %copy-done.8, f32[6,1,512,128]{3,2,1,0:T(8,128)S(1)} %copy-done, s32[1,512,128]{2,1,0:T(8,128)S(1)} %copy-done.2, ...), custom_call_target="tpu_custom_call" | custom-call | bytes 15000000 | tf_op jit(solution)/shard_map/pallas_call | solution.py:308
  27.0 1.0 %collective-permute-start.3 = (f32[4,128]{1,0:T(4,128)S(1)}, f32[4,128]{1,0:T(4,128)S(1)}, u32[]{:S(2)}, u32[]{:S(2)}) collective-permute-start(f32[4,128]{1,0:T(4,128)S(1)} %get-tuple-element.7), channel_id=1, source_target_pairs={{0,64},{64,0},{1,65},{65,1},{2,66},{66,2},{3,67},{67,3},{4,68},{68... | collective-permute-start | bytes 6152 | tf_op jit(solution)/shard_map/ppermute | solution.py:254
  27.9 0.0 collective-permute-done.arrived
  27.9 0.8 %shard_map.90.held = f32[6,1,768,128]{3,2,1,0:T(8,128)} custom-call(f32[6,1,768,128]{3,2,1,0:T(8,128)} %get-tuple-element.5.held, f32[6,128,128]{2,1,0:T(8,128)S(1)} %collective-permute-done.arrived), custom_call_target="tpu_custom_call", output_to_operand_aliasing={{}: (0, {})} | custom-call | tf_op jit(solution)/shard_map/pallas_call | solution.py:333
  28.7 0.0 collective-permute-done.3.arrived
  28.7 1.8 %collective-permute-done.2.velocity = f32[3,128,128]{2,1,0:T(8,128)S(1)} collective-permute-done((f32[3,128,128]{2,1,0:T(8,128)S(1)}, f32[3,128,128]{2,1,0:T(8,128)S(1)}, u32[]{:S(2)}, u32[]{:S(2)}) %collective-permute-start.2) | collective-permute-done | bytes 196640 | tf_op jit(solution)/shard_map/ppermute | solution.py:254
  30.5 4.2 %collective-permute-done.1.position = f32[3,128,128]{2,1,0:T(8,128)S(1)} collective-permute-done((f32[3,128,128]{2,1,0:T(8,128)S(1)}, f32[3,128,128]{2,1,0:T(8,128)S(1)}, u32[]{:S(2)}, u32[]{:S(2)}) %collective-permute-start.1) | collective-permute-done | bytes 196640 | tf_op jit(solution)/shard_map/ppermute | solution.py:254
  34.7 0.8 %shard_map.91 = (f32[6,1,768,128]{3,2,1,0:T(8,128)}, f32[4,1,128]{2,1,0:T(1,128)}) custom-call(f32[6,1,768,128]{3,2,1,0:T(8,128)} %shard_map.90.held, f32[3,128,128]{2,1,0:T(8,128)S(1)} %collective-permute-done.1.position, f32[3,128,128]{2,1,0:T(8,128)S(1)} %collective-permute-done.2.velocity, ...), custom_call_target="tpu_custom_call", output_to_operand_aliasing={{0}: (0, {})} | custom-call | tf_op jit(solution)/shard_map/pallas_call | solution.py:341
Async XLA Ops:
  1.4 1.4 %copy-start = (f32[6,1,512,128]{3,2,1,0:T(8,128)S(1)}, f32[6,1,512,128]{3,2,1,0:T(8,128)}, u32[]{:S(2)}) copy-start(f32[6,1,512,128]{3,2,1,0:T(8,128)} %particles.3) | copy-start | bytes 4718596
  2.8 0.7 %copy-start.7 = (s32[1,512]{1,0:T(1,128)S(1)}, s32[1,512]{1,0:T(1,128)}, u32[]{:S(2)}) copy-start(s32[1,512]{1,0:T(1,128)} %destination.7) | copy-start | bytes 6148
  3.5 5.3 %copy-start.2 = (s32[1,512,128]{2,1,0:T(8,128)S(1)}, s32[1,512,128]{2,1,0:T(8,128)}, u32[]{:S(2)}) copy-start(s32[1,512,128]{2,1,0:T(8,128)} %order.5) | copy-start | bytes 786436
  3.5 5.3 %copy-start.4 = (s32[1,512,64]{1,2,0:T(8,128)S(1)}, s32[1,512,64]{1,2,0:T(8,128)}, u32[]{:S(2)}) copy-start(s32[1,512,64]{1,2,0:T(8,128)} %param.9) | copy-start | bytes 393220
  3.5 5.3 %copy-start.6 = (s32[1,512,64]{1,2,0:T(8,128)S(1)}, s32[1,512,64]{1,2,0:T(8,128)}, u32[]{:S(2)}) copy-start(s32[1,512,64]{1,2,0:T(8,128)} %param.10) | copy-start | bytes 393220
  4.5 1.0 %copy-start.1 = (s32[1,512,128]{2,1,0:T(8,128)S(1)}, s32[1,512,128]{2,1,0:T(8,128)}, u32[]{:S(2)}) copy-start(s32[1,512,128]{2,1,0:T(8,128)} %order.5) | copy-start | bytes 786436
  5.5 0.9 %copy-start.3 = (s32[1,512,64]{1,2,0:T(8,128)S(1)}, s32[1,512,64]{1,2,0:T(8,128)}, u32[]{:S(2)}) copy-start(s32[1,512,64]{1,2,0:T(8,128)} %param.9) | copy-start | bytes 393220
  6.4 0.9 %copy-start.5 = (s32[1,512,64]{1,2,0:T(8,128)S(1)}, s32[1,512,64]{1,2,0:T(8,128)}, u32[]{:S(2)}) copy-start(s32[1,512,64]{1,2,0:T(8,128)} %param.10) | copy-start | bytes 393220
  7.3 12.4 %copy-start.8 = (s32[1,512]{1,0:T(1,128)S(1)}, s32[1,512]{1,0:T(1,128)}, u32[]{:S(2)}) copy-start(s32[1,512]{1,0:T(1,128)} %cells.1) | copy-start | bytes 6148
  10.3 17.6 %collective-permute-start = (f32[6,128,128]{2,1,0:T(8,128)S(1)}, f32[6,128,128]{2,1,0:T(8,128)S(1)}, u32[]{:S(2)}, u32[]{:S(2)}) collective-permute-start(f32[6,128,128]{2,1,0:T(8,128)S(1)} %shard_map.88.sent), channel_id=1, source_target_pairs={{0,63},{1,0},{2,1},{3,2},{4,3},{5,4},{6,5},{7,6},{8,7},{9,8},{10,9... | collective-permute-start | bytes 1179656 | tf_op jit(solution)/shard_map/ppermute | solution.py:254
  19.6 10.9 %collective-permute-start.2 = (f32[3,128,128]{2,1,0:T(8,128)S(1)}, f32[3,128,128]{2,1,0:T(8,128)S(1)}, u32[]{:S(2)}, u32[]{:S(2)}) collective-permute-start(f32[3,128,128]{2,1,0:T(8,128)S(1)} %shard_map.87.sent), channel_id=1, source_target_pairs={{0,1},{1,2},{2,3},{3,4},{4,5},{5,6},{6,7},{7,8},{8,9},{9,10},{10,1... | collective-permute-start | bytes 589832 | tf_op jit(solution)/shard_map/ppermute | solution.py:254
  19.6 15.1 %collective-permute-start.1 = (f32[3,128,128]{2,1,0:T(8,128)S(1)}, f32[3,128,128]{2,1,0:T(8,128)S(1)}, u32[]{:S(2)}, u32[]{:S(2)}) collective-permute-start(f32[3,128,128]{2,1,0:T(8,128)S(1)} %shard_map.86.sent), channel_id=1, source_target_pairs={{0,1},{1,2},{2,3},{3,4},{4,5},{5,6},{6,7},{7,8},{8,9},{9,10},{10,1... | collective-permute-start | bytes 589832 | tf_op jit(solution)/shard_map/ppermute | solution.py:254
  27.0 1.8 %collective-permute-start.3 = (f32[4,128]{1,0:T(4,128)S(1)}, f32[4,128]{1,0:T(4,128)S(1)}, u32[]{:S(2)}, u32[]{:S(2)}) collective-permute-start(f32[4,128]{1,0:T(4,128)S(1)} %get-tuple-element.7), channel_id=1, source_target_pairs={{0,64},{64,0},{1,65},{65,1},{2,66},{66,2},{3,67},{67,3},{4,68},{68... | collective-permute-start | bytes 6152 | tf_op jit(solution)/shard_map/ppermute | solution.py:254

commit v2 on v1

--- a/solution.py
+++ b/solution.py
@@ -154,43 +154,49 @@
     return jnp.where(ranking == rows, 1.0, 0.0).astype(jnp.bfloat16)
 
 
-def position_kernel(scalars, destination, position, out):
-    selection = mover_selection(destination[...], scalars[0], scalars[1])
-    for c in range(3):
-        out[c] = pick(selection, position[c, 0])
-
-
-def movers_collided(scalars, at, destination, velocity, order, accepted, direction):
-    selection = mover_selection(destination[...], scalars[0], scalars[at])
-    info = jnp.where(accepted[0] == 1, direction[0], -1).astype(jnp.float32).astype(jnp.bfloat16)
+def place_on_mesh():
+    return lax.axis_index("space"), lax.axis_index("rep")
+
+
+def neighbour(steps):
+    slab, _ = place_on_mesh()
+    return lax.rem(slab + SLABS + steps, SLABS)
+
+
+def movers_kernel(steps, live, destination, particles, order, accepted, direction, sent, out, data, orders, takens, turns, sems):
+    del sent
+    copies = [
+        pltpu.make_async_copy(order, orders, sems.at[0]),
+        pltpu.make_async_copy(accepted, takens, sems.at[1]),
+        pltpu.make_async_copy(direction, turns, sems.at[2]),
+        pltpu.make_async_copy(particles.at[3:6], data.at[3:6], sems.at[3]),
+        pltpu.make_async_copy(particles.at[0:3], data.at[0:3], sems.at[4]),
+    ]
+    for c in copies:
+        c.start()
+    selection = mover_selection(destination[...], live[0, 0], neighbour(steps))
+    for c in copies[:3]:
+        c.wait()
+    info = jnp.where(takens[0] == 1, turns[0], -1).astype(jnp.float32).astype(jnp.bfloat16)
     chosen = dot_lanes(info, selection)
-    orders = dot(selection, order[0].astype(jnp.float32).astype(jnp.bfloat16))
-    codes = partner_codes(orders.T, chosen).T.astype(jnp.int32)
-    return selection, collide([pick(selection, velocity[c, 0]) for c in range(3)], codes)
-
-
-def upward_kernel(scalars, destination, velocity, order, accepted, direction, sent, out):
-    del sent
-    _, result = movers_collided(scalars, 1, destination, velocity, order, accepted, direction)
-    for c in range(3):
-        out[c] = result[c]
-
-
-def downward_kernel(scalars, destination, particles, order, accepted, direction, sent, out):
-    del sent
-    velocity = particles.at[3:6]
-    selection, result = movers_collided(scalars, 2, destination, velocity, order, accepted, direction)
+    codes = partner_codes(dot(selection, orders[0].astype(jnp.float32).astype(jnp.bfloat16)).T, chosen)
+    copies[3].wait()
+    velocity = [pick(selection, data[3 + c, 0]) for c in range(3)]
+    copies[4].wait()
+    position = [pick(selection, data[c, 0]) for c in range(3)]
+    result = collide(velocity, codes.T.astype(jnp.int32))
     for c in range(3):
         out[3 + c] = result[c]
-        out[c] = pick(selection, particles[c, 0]) + time_step * result[c]
-
-
-def own_kernel(scalars, destination, cells, particles, order, accepted, direction, sent, moved, mine, theirs, total):
+        out[c] = position[c] + time_step * result[c]
+
+
+def own_kernel(live_count, destination, cells, particles, order, accepted, direction, sent, moved, mine, theirs, total):
     del sent
     step = pl.program_id(0)
     slots = lax.broadcasted_iota(jnp.int32, (1, PART), 1) + step * PART
-    live = slots < scalars[0]
-    staying = jnp.where(live & (destination[...] == scalars[3]), 1.0, 0.0)
+    slab, rep = place_on_mesh()
+    live = slots < live_count[0, 0]
+    staying = jnp.where(live & (destination[...] == slab), 1.0, 0.0)
     info = jnp.where(accepted[0] == 1, direction[0], -1).astype(jnp.float32)
     codes = partner_codes(order[0].astype(jnp.float32).T, info) + staying * 8388608.0
     codes = codes.T.astype(jnp.int32)
@@ -199,7 +205,7 @@
     for c in range(3):
         moved[3 + c, 0] = jnp.where(keep, result[c], 0.0)
         moved[c, 0] = jnp.where(keep, particles[c, 0] + time_step * result[c], 0.0)
-    cell = (cells[...] + scalars[4] * (CELLS // 2)) & (CELLS - 1)
+    cell = (cells[...] + rep * (CELLS // 2)) & (CELLS - 1)
     cell = jnp.where(live, cell, -1)
     onehot = lax.broadcasted_iota(jnp.int32, (CELLS, PART), 0) == cell
     onehot = jnp.where(onehot, 1.0, 0.0).astype(jnp.bfloat16)
@@ -230,12 +236,9 @@
     moved[:, 0] = arrived[...]
 
 
-def above_kernel(held, position, velocity, mine, arrived, moved, samples, *, parts):
+def above_kernel(parts, held, up, mine, arrived, moved, samples):
     del held
-    for c in range(3):
-        v = velocity[c]
-        moved[3 + c, 0] = v
-        moved[c, 0] = position[c] + time_step * v
+    moved[:, 0] = up[...]
     samples[:, 0] = (mine[...] + arrived[...]) * (1.0 / (PART * parts))
 
 
@@ -257,50 +260,29 @@
 def per_device(particles, pair_order, accepted, direction, destination, live_count, cell_index):
     accepted = jnp.swapaxes(accepted, 1, 2)
     direction = jnp.swapaxes(direction, 1, 2)
-    slab = lax.axis_index("space")
-    total = lax.axis_size("space")
-    rep = lax.axis_index("rep")
     parts = lax.axis_size("rep")
-    scalars = jnp.stack([live_count[0, 0], (slab + 1) % total, (slab + total - 1) % total, slab, rep]).astype(jnp.int32)
     f32 = jnp.float32
-    limit = pltpu.CompilerParams(vmem_limit_bytes=40 * 2**20)
+    limit = pltpu.CompilerParams(vmem_limit_bytes=56 * 2**20)
     once = dict(grid=(1,), compiler_params=limit)
 
-    def cost(microseconds):
-        return pl.CostEstimate(flops=0, bytes_accessed=int(microseconds * 3.0e6), transcendentals=0)
-
-
-    row = whole((1, CAP))
-    up_position = pl.pallas_call(
-        position_kernel,
-        in_specs=[SMEM, row, whole((3, 1, CAP, PART))],
-        out_specs=whole((3, MOVE, PART)),
-        out_shape=jax.ShapeDtypeStruct((3, MOVE, PART), f32),
-        cost_estimate=cost(1),
-        **once,
-    )(scalars, destination, particles)
-    position_from_lower = from_behind(up_position, "space", 1)
-
-    pair_specs = [whole((1, CAP, PART)), whole((1, PAIRS, CAP)), whole((1, PAIRS, CAP)), ANY]
-    up_velocity = pl.pallas_call(
-        upward_kernel,
-        in_specs=[SMEM, row, whole((3, 1, CAP, PART), (1, 0, 0, 0)), *pair_specs],
-        out_specs=whole((3, MOVE, PART)),
-        out_shape=jax.ShapeDtypeStruct((3, MOVE, PART), f32),
-        cost_estimate=cost(2),
-        **once,
-    )(scalars, destination, particles, pair_order, accepted, direction, up_position)
-    velocity_from_lower = from_behind(up_velocity, "space", 1)
-
-    down = pl.pallas_call(
-        downward_kernel,
-        in_specs=[SMEM, row, whole((6, 1, CAP, PART)), *pair_specs],
-        out_specs=whole((6, MOVE, PART)),
-        out_shape=jax.ShapeDtypeStruct((6, MOVE, PART), f32),
-        cost_estimate=cost(2),
-        **once,
-    )(scalars, destination, particles, pair_order, accepted, direction, up_velocity)
-    from_upper = from_behind(down, "space", -1)
+    def movers(steps, after):
+        return pl.pallas_call(
+            functools.partial(movers_kernel, steps),
+            in_specs=[SMEM, whole((1, CAP)), ANY, ANY, ANY, ANY, ANY],
+            out_specs=whole((6, MOVE, PART)),
+            out_shape=jax.ShapeDtypeStruct((6, MOVE, PART), f32),
+            scratch_shapes=[
+                pltpu.VMEM((6, 1, CAP, PART), f32),
+                pltpu.VMEM((1, CAP, PART), jnp.int32),
+                pltpu.VMEM((1, PAIRS, CAP), jnp.int32),
+                pltpu.VMEM((1, PAIRS, CAP), jnp.int32),
+                pltpu.SemaphoreType.DMA((5,)),
+            ],
+            **once,
+        )(live_count, destination, particles, pair_order, accepted, direction, after)
+
+    up = movers(1, live_count)
+    from_lower = from_behind(up, "space", 1)
 
     lanes = pl.BlockSpec((1, PART), lambda i: (0, i))
     pairs = pl.BlockSpec((1, PAIRS, PART), lambda i: (0, 0, i))
@@ -325,27 +307,29 @@
         ],
         out_shape=[jax.ShapeDtypeStruct((6, 1, OUTCAP, PART), f32), half, half],
         scratch_shapes=[pltpu.VMEM((4, CELLS, PART), f32)],
-        cost_estimate=cost(5),
         compiler_params=limit,
-    )(scalars, destination, cell_index, particles, pair_order, accepted, direction, down)
+    )(live_count, destination, cell_index, particles, pair_order, accepted, direction, up)
     arrived = from_behind(theirs, "rep", 1)
-
+    from_upper = from_behind(movers(-1, mine), "space", -1)
+
+    moved, samples = pl.pallas_call(
+        functools.partial(above_kernel, parts),
+        in_specs=[ANY, whole((6, MOVE, PART)), whole((4, CELLS // 2)), whole((4, CELLS // 2))],
+        out_specs=[whole((6, 1, MOVE, PART)), whole((4, 1, CELLS // 2))],
+        out_shape=[jax.ShapeDtypeStruct(moved.shape, f32), jax.ShapeDtypeStruct((4, 1, CELLS // 2), f32)],
+        input_output_aliases={0: 0},
+        grid=(1,),
+        compiler_params=pltpu.CompilerParams(vmem_limit_bytes=8 * 2**20),
+    )(moved, from_lower, mine, arrived)
     moved = pl.pallas_call(
         below_kernel,
         in_specs=[ANY, whole((6, MOVE, PART))],
         out_specs=whole((6, 1, MOVE, PART), (0, 0, 5, 0)),
         out_shape=jax.ShapeDtypeStruct(moved.shape, f32),
         input_output_aliases={0: 0},
-        **once,
+        grid=(1,),
+        compiler_params=pltpu.CompilerParams(vmem_limit_bytes=8 * 2**20),
     )(moved, from_upper)
-    moved, samples = pl.pallas_call(
-        functools.partial(above_kernel, parts=parts),
-        in_specs=[ANY, whole((3, MOVE, PART)), whole((3, MOVE, PART)), whole((4, CELLS // 2)), whole((4, CELLS // 2))],
-        out_specs=[whole((6, 1, MOVE, PART)), whole((4, 1, CELLS // 2))],
-        out_shape=[jax.ShapeDtypeStruct(moved.shape, f32), jax.ShapeDtypeStruct((4, 1, CELLS // 2), f32)],
-        input_output_aliases={0: 0},
-        **once,
-    )(moved, position_from_lower, velocity_from_lower, mine, arrived)
     return (moved, samples)
 
 

time: 36.2 us -> 35.1 us (0.970)
  local copies, waits for them, and re-layouts: 4.94 us -> 0.01 us
  Pallas kernels: 12.9 us -> 16.7 us
    unnamed x18 -> x4, local copies, waits for them, and re-layouts: 4.86 us -> 0.01 us
    pallas_call x4 -> x3, Pallas kernels: 4.82 us -> 8.27 us  [the longest x2 7.49 us: movers(): pl.pallas_call(functools.partial(movers_kernel, steps), in_specs=[SMEM, w...]
    pallas_call x1, Pallas kernels: 7.31 us -> 7.68 us  [per_device(): pl.pallas_call(own_kernel, grid=(CAP // PART,), in_specs=[SMEM, lanes, la...]
    ppermute x4 -> x3, waiting for transfers between devices: 6.04 us -> 6.36 us  [from_behind(): return lax.ppermute(value, axis, pairs)]
    ppermute x4 -> x3, starting transfers between devices: 10.3 us -> 10.4 us  [from_behind(): return lax.ppermute(value, axis, pairs)]
  transfers between devices with their start and end apart: 4 -> 3, of which waited for: 2 -> 2; matrix products, arithmetic and copies ran while one was open for 0% -> 0% of each run, Pallas kernels for 23% -> 35%
where the time goes in v2:
time: 35.1 us; the launch traced here: 34.8 us
  Pallas kernels  16.7 us (48%)
  starting transfers between devices  10.4 us (30%)
  waiting for transfers between devices  6.36 us (18%)
  between operations  1.3 us (4%)
    ppermute x3, starting transfers between devices, from_behind(): return lax.ppermute(value, axis, pairs)  10.4 us
    pallas_call x1, Pallas kernels, per_device(): pl.pallas_call(own_kernel, grid=(CAP // PART,), in_specs=[SMEM, lanes, la...  7.68 us
    pallas_call x2, Pallas kernels, movers(): pl.pallas_call(functools.partial(movers_kernel, steps), in_specs=[SMEM, w...  7.49 us
    ppermute x3, waiting for transfers between devices, from_behind(): return lax.ppermute(value, axis, pairs)  6.36 us
    pallas_call x1, Pallas kernels, per_device(): pl.pallas_call(functools.partial(above_kernel, parts), in_specs=[ANY, who...  0.78 us
    pallas_call x1, Pallas kernels, per_device(): pl.pallas_call(below_kernel, in_specs=[ANY, whole((6, MOVE, PART))], out_...  0.77 us
  transfers between devices with their start and end apart: 3, of which 2 were waited for; matrix products, arithmetic and copies ran while one was open for 0% of the time, Pallas kernels for 35%

profile of v2, /device:TPU:1, one launch (start us, length us, event | category | flops | bytes accessed | tf_op | source)
XLA Modules:
  0.0 34.8 jit_solution(15598475168923914733)
XLA Ops:
  1.3 3.7 %shard_map.86.sent = f32[6,128,128]{2,1,0:T(8,128)} custom-call(s32[1,1]{1,0:T(1,128)S(6)} %copy.13.live.sent.live_count, s32[1,512]{1,0:T(1,128)} %destination.5, f32[6,1,512,128]{3,2,1,0:T(8,128)} %particles.5, s32[1,512,128]{2,1,0:T(8,128)} %order.5, s32[1,64,512]{2,1,0:T(8,128)} %bitcast.2, s32[1,64,512]{2,1,0:T(8,128)} %bitcast.5, ...), custom_call_target="tpu_custom_call" | custom-call | tf_op jit(solution)/shard_map/pallas_call | solution.py:269
  5.0 2.1 %collective-permute-start = (f32[6,128,128]{2,1,0:T(8,128)}, f32[6,128,128]{2,1,0:T(8,128)S(1)}, u32[]{:S(2)}, u32[]{:S(2)}) collective-permute-start(f32[6,128,128]{2,1,0:T(8,128)} %shard_map.86.sent), channel_id=1, source_target_pairs={{0,1},{1,2},{2,3},{3,4},{4,5},{5,6},{6,7},{7,8},{8,9},{9,10},{10,1... | collective-permute-start | bytes 1179656 | tf_op jit(solution)/shard_map/ppermute | solution.py:257
  7.1 7.7 %shard_map.87 = (f32[6,1,768,128]{3,2,1,0:T(8,128)}, f32[4,128]{1,0:T(4,128)}, f32[4,128]{1,0:T(4,128)}) custom-call(s32[1,1]{1,0:T(1,128)S(6)} %copy.13.live.sent.live_count, s32[1,512]{1,0:T(1,128)} %destination.5, s32[1,512]{1,0:T(1,128)} %cells.1, f32[6,1,512,128]{3,2,1,0:T(8,128)} %particles.5, s32[1,512,128]{2,1,0:T(8,128)} %order.5, ...), custom_call_target="tpu_custom_call" | custom-call | tf_op jit(solution)/shard_map/pallas_call | solution.py:290
  14.8 0.0 copy-start.1
  14.8 0.0 copy-start
  14.8 3.7 %shard_map.89 = f32[6,128,128]{2,1,0:T(8,128)} custom-call(s32[1,1]{1,0:T(1,128)S(6)} %copy.13.live.sent.live_count, s32[1,512]{1,0:T(1,128)} %destination.5, f32[6,1,512,128]{3,2,1,0:T(8,128)} %particles.5, s32[1,512,128]{2,1,0:T(8,128)} %order.5, s32[1,64,512]{2,1,0:T(8,128)} %bitcast.4, s32[1,64,512]{2,1,0:T(8,128)} %bitcast.7, ...), custom_call_target="tpu_custom_call" | custom-call | tf_op jit(solution)/shard_map/pallas_call | solution.py:269
  18.6 7.3 %collective-permute-start.2 = (f32[6,128,128]{2,1,0:T(8,128)}, f32[6,128,128]{2,1,0:T(8,128)S(1)}, u32[]{:S(2)}, u32[]{:S(2)}) collective-permute-start(f32[6,128,128]{2,1,0:T(8,128)} %shard_map.89), channel_id=1, source_target_pairs={{0,63},{1,0},{2,1},{3,2},{4,3},{5,4},{6,5},{7,6},{8,7},{9,8},{10,9... | collective-permute-start | bytes 1179656 | tf_op jit(solution)/shard_map/ppermute | solution.py:257
  25.9 0.0 copy-done.1
  25.9 1.0 %collective-permute-start.1 = (f32[4,128]{1,0:T(4,128)S(1)}, f32[4,128]{1,0:T(4,128)S(1)}, u32[]{:S(2)}, u32[]{:S(2)}) collective-permute-start(f32[4,128]{1,0:T(4,128)S(1)} %copy-done.1), channel_id=1, source_target_pairs={{0,64},{64,0},{1,65},{65,1},{2,66},{66,2},{3,67},{67,3},{4,68},{68... | collective-permute-start | bytes 6152 | tf_op jit(solution)/shard_map/ppermute | solution.py:257
  26.8 0.8 %collective-permute-done.1.arrived = f32[4,128]{1,0:T(4,128)S(1)} collective-permute-done((f32[4,128]{1,0:T(4,128)S(1)}, f32[4,128]{1,0:T(4,128)S(1)}, u32[]{:S(2)}, u32[]{:S(2)}) %collective-permute-start.1) | collective-permute-done | bytes 2080 | tf_op jit(solution)/shard_map/ppermute | solution.py:257
  27.7 0.0 collective-permute-done.up
  27.7 0.0 copy-done
  27.7 0.8 %shard_map.88 = (f32[6,1,768,128]{3,2,1,0:T(8,128)}, f32[4,1,128]{2,1,0:T(1,128)}) custom-call(f32[6,1,768,128]{3,2,1,0:T(8,128)} %get-tuple-element.7.held, f32[6,128,128]{2,1,0:T(8,128)S(1)} %collective-permute-done.up, f32[4,128]{1,0:T(4,128)S(1)} %copy-done, f32[4,128]{1,0:T(4,128)S(1)} %collective-permute-done.1.arrived), custom_call_target="tpu_custom_call", output_to_operand_aliasing={{0}: (0, {})} | custom-call | tf_op jit(solution)/shard_map/pallas_call | solution.py:315
  28.4 5.5 %collective-permute-done.2.arrived = f32[6,128,128]{2,1,0:T(8,128)S(1)} collective-permute-done((f32[6,128,128]{2,1,0:T(8,128)}, f32[6,128,128]{2,1,0:T(8,128)S(1)}, u32[]{:S(2)}, u32[]{:S(2)}) %collective-permute-start.2) | collective-permute-done | bytes 393248 | tf_op jit(solution)/shard_map/ppermute | solution.py:257
  34.0 0.8 %shard_map.90 = f32[6,1,768,128]{3,2,1,0:T(8,128)} custom-call(f32[6,1,768,128]{3,2,1,0:T(8,128)} %get-tuple-element.10.held, f32[6,128,128]{2,1,0:T(8,128)S(1)} %collective-permute-done.2.arrived), custom_call_target="tpu_custom_call", output_to_operand_aliasing={{}: (0, {})} | custom-call | tf_op jit(solution)/shard_map/pallas_call | solution.py:324
Async XLA Ops:
  5.0 22.6 %collective-permute-start = (f32[6,128,128]{2,1,0:T(8,128)}, f32[6,128,128]{2,1,0:T(8,128)S(1)}, u32[]{:S(2)}, u32[]{:S(2)}) collective-permute-start(f32[6,128,128]{2,1,0:T(8,128)} %shard_map.86.sent), channel_id=1, source_target_pairs={{0,1},{1,2},{2,3},{3,4},{4,5},{5,6},{6,7},{7,8},{8,9},{9,10},{10,1... | collective-permute-start | bytes 1179656 | tf_op jit(solution)/shard_map/ppermute | solution.py:257
  14.8 11.1 %copy-start.1 = (f32[4,128]{1,0:T(4,128)S(1)}, f32[4,128]{1,0:T(4,128)}, u32[]{:S(2)}) copy-start(f32[4,128]{1,0:T(4,128)} %get-tuple-element.9) | copy-start | bytes 6148
  14.8 12.8 %copy-start = (f32[4,128]{1,0:T(4,128)S(1)}, f32[4,128]{1,0:T(4,128)}, u32[]{:S(2)}) copy-start(f32[4,128]{1,0:T(4,128)} %get-tuple-element.8.mine.sent) | copy-start | bytes 6148
  18.6 15.4 %collective-permute-start.2 = (f32[6,128,128]{2,1,0:T(8,128)}, f32[6,128,128]{2,1,0:T(8,128)S(1)}, u32[]{:S(2)}, u32[]{:S(2)}) collective-permute-start(f32[6,128,128]{2,1,0:T(8,128)} %shard_map.89), channel_id=1, source_target_pairs={{0,63},{1,0},{2,1},{3,2},{4,3},{5,4},{6,5},{7,6},{8,7},{9,8},{10,9... | collective-permute-start | bytes 1179656 | tf_op jit(solution)/shard_map/ppermute | solution.py:257
  25.9 1.8 %collective-permute-start.1 = (f32[4,128]{1,0:T(4,128)S(1)}, f32[4,128]{1,0:T(4,128)S(1)}, u32[]{:S(2)}, u32[]{:S(2)}) collective-permute-start(f32[4,128]{1,0:T(4,128)S(1)} %copy-done.1), channel_id=1, source_target_pairs={{0,64},{64,0},{1,65},{65,1},{2,66},{66,2},{3,67},{67,3},{4,68},{68... | collective-permute-start | bytes 6152 | tf_op jit(solution)/shard_map/ppermute | solution.py:257

commit v3 on v2

--- a/solution.py
+++ b/solution.py
@@ -143,15 +143,15 @@
     return dot(selection, high) + dot(selection, low)
 
 
-def mover_selection(destination, live, target):
-    slots = lax.broadcasted_iota(jnp.int32, (1, CAP), 1)
-    moving = (slots < live) & (destination == target)
+def mover_selection(destination):
+    up = destination == neighbour(1)
+    down = destination == neighbour(-1)
     ahead = lax.broadcasted_iota(jnp.int32, (CAP, CAP), 0) < lax.broadcasted_iota(jnp.int32, (CAP, CAP), 1)
-    flags = jnp.broadcast_to(jnp.where(moving, 1.0, 0.0), (8, CAP))
-    ranking = dot(flags.astype(jnp.bfloat16), jnp.where(ahead, 1.0, 0.0).astype(jnp.bfloat16))[:1]
-    ranking = jnp.where(moving, ranking, -1.0)
+    flags = jnp.concatenate([jnp.where(up, 1.0, 0.0), jnp.where(down, 1.0, 0.0), jnp.zeros((6, CAP), jnp.float32)], axis=0)
+    ranking = dot(flags.astype(jnp.bfloat16), jnp.where(ahead, 1.0, 0.0).astype(jnp.bfloat16))
     rows = lax.broadcasted_iota(jnp.int32, (MOVE, CAP), 0).astype(jnp.float32)
-    return jnp.where(ranking == rows, 1.0, 0.0).astype(jnp.bfloat16)
+    chosen = [rows == jnp.where(moving, ranking[i : i + 1], -1.0) for i, moving in enumerate((up, down))]
+    return jnp.where(jnp.concatenate(chosen, axis=0), 1.0, 0.0).astype(jnp.bfloat16)
 
 
 def place_on_mesh():
@@ -163,31 +163,45 @@
     return lax.rem(slab + SLABS + steps, SLABS)
 
 
-def movers_kernel(steps, live, destination, particles, order, accepted, direction, sent, out, data, orders, takens, turns, sems):
-    del sent
+def movers_kernel(
+    destination, order, accepted, direction, particles, up, down, targets, orders, takens, turns, data, sems
+):
     copies = [
-        pltpu.make_async_copy(order, orders, sems.at[0]),
-        pltpu.make_async_copy(accepted, takens, sems.at[1]),
-        pltpu.make_async_copy(direction, turns, sems.at[2]),
-        pltpu.make_async_copy(particles.at[3:6], data.at[3:6], sems.at[3]),
-        pltpu.make_async_copy(particles.at[0:3], data.at[0:3], sems.at[4]),
+        pltpu.make_async_copy(source, target, sems.at[i])
+        for i, (source, target) in enumerate(
+            (
+                (destination, targets),
+                (order, orders),
+                (accepted, takens),
+                (direction, turns),
+                (particles.at[3:6], data.at[3:6]),
+                (particles.at[0:3], data.at[0:3]),
+            )
+        )
     ]
     for c in copies:
         c.start()
-    selection = mover_selection(destination[...], live[0, 0], neighbour(steps))
-    for c in copies[:3]:
+    copies[0].wait()
+    selection = mover_selection(targets[...])
+    for c in copies[1:4]:
         c.wait()
     info = jnp.where(takens[0] == 1, turns[0], -1).astype(jnp.float32).astype(jnp.bfloat16)
     chosen = dot_lanes(info, selection)
-    codes = partner_codes(dot(selection, orders[0].astype(jnp.float32).astype(jnp.bfloat16)).T, chosen)
-    copies[3].wait()
+    order_rows = dot(selection, orders[0].astype(jnp.float32).astype(jnp.bfloat16))
+    codes = []
+    for i in range(2):
+        part = slice(i * MOVE, (i + 1) * MOVE)
+        codes.append(partner_codes(order_rows[part].T, chosen[:, part]).T.astype(jnp.int32))
+    copies[4].wait()
     velocity = [pick(selection, data[3 + c, 0]) for c in range(3)]
-    copies[4].wait()
+    copies[5].wait()
     position = [pick(selection, data[c, 0]) for c in range(3)]
-    result = collide(velocity, codes.T.astype(jnp.int32))
-    for c in range(3):
-        out[3 + c] = result[c]
-        out[c] = position[c] + time_step * result[c]
+    for i, out in enumerate((up, down)):
+        part = slice(i * MOVE, (i + 1) * MOVE)
+        result = collide([v[part] for v in velocity], codes[i])
+        for c in range(3):
+            out[3 + c] = result[c]
+            out[c] = position[c][part] + time_step * result[c]
 
 
 def own_kernel(live_count, destination, cells, particles, order, accepted, direction, sent, moved, mine, theirs, total):
@@ -231,15 +245,17 @@
             theirs[c : c + 1] = sums[:1, CELLS // 2 :]
 
 
-def below_kernel(held, arrived, moved):
+def arrivals_kernel(parts, held, below, above, mine, arrived, moved, samples, sems):
     del held
-    moved[:, 0] = arrived[...]
-
-
-def above_kernel(parts, held, up, mine, arrived, moved, samples):
-    del held
-    moved[:, 0] = up[...]
+    copies = [
+        pltpu.make_async_copy(below, moved.at[:, 0, 0:MOVE], sems.at[0]),
+        pltpu.make_async_copy(above, moved.at[:, 0, MOVE + CAP : OUTCAP], sems.at[1]),
+    ]
+    for c in copies:
+        c.start()
     samples[:, 0] = (mine[...] + arrived[...]) * (1.0 / (PART * parts))
+    for c in copies:
+        c.wait()
 
 
 def whole(shape, at=None):
@@ -248,7 +264,8 @@
 
 
 SMEM = pl.BlockSpec(memory_space=pltpu.SMEM)
-ANY = pl.BlockSpec(memory_space=pl.ANY)
+VMEM = pl.BlockSpec(memory_space=pltpu.VMEM)
+HBM = pl.BlockSpec(memory_space=pltpu.HBM)
 
 
 def from_behind(value, axis, steps):
@@ -263,26 +280,25 @@
     parts = lax.axis_size("rep")
     f32 = jnp.float32
     limit = pltpu.CompilerParams(vmem_limit_bytes=56 * 2**20)
-    once = dict(grid=(1,), compiler_params=limit)
-
-    def movers(steps, after):
-        return pl.pallas_call(
-            functools.partial(movers_kernel, steps),
-            in_specs=[SMEM, whole((1, CAP)), ANY, ANY, ANY, ANY, ANY],
-            out_specs=whole((6, MOVE, PART)),
-            out_shape=jax.ShapeDtypeStruct((6, MOVE, PART), f32),
-            scratch_shapes=[
-                pltpu.VMEM((6, 1, CAP, PART), f32),
-                pltpu.VMEM((1, CAP, PART), jnp.int32),
-                pltpu.VMEM((1, PAIRS, CAP), jnp.int32),
-                pltpu.VMEM((1, PAIRS, CAP), jnp.int32),
-                pltpu.SemaphoreType.DMA((5,)),
-            ],
-            **once,
-        )(live_count, destination, particles, pair_order, accepted, direction, after)
-
-    up = movers(1, live_count)
+
+    sent = jax.ShapeDtypeStruct((6, MOVE, PART), f32)
+    up, down = pl.pallas_call(
+        movers_kernel,
+        in_specs=[HBM] * 5,
+        out_specs=[VMEM, VMEM],
+        out_shape=[sent, sent],
+        scratch_shapes=[
+            pltpu.VMEM((1, CAP), jnp.int32),
+            pltpu.VMEM((1, CAP, PART), jnp.int32),
+            pltpu.VMEM((1, PAIRS, CAP), jnp.int32),
+            pltpu.VMEM((1, PAIRS, CAP), jnp.int32),
+            pltpu.VMEM((6, 1, CAP, PART), f32),
+            pltpu.SemaphoreType.DMA((6,)),
+        ],
+        compiler_params=limit,
+    )(destination, pair_order, accepted, direction, particles)
     from_lower = from_behind(up, "space", 1)
+    from_upper = from_behind(down, "space", -1)
 
     lanes = pl.BlockSpec((1, PART), lambda i: (0, i))
     pairs = pl.BlockSpec((1, PAIRS, PART), lambda i: (0, 0, i))
@@ -298,7 +314,7 @@
             pl.BlockSpec((1, PART, PART), lambda i: (0, i, 0)),
             pairs,
             pairs,
-            ANY,
+            HBM,
         ],
         out_specs=[
             pl.BlockSpec((6, 1, PART, PART), lambda i: (0, 0, i + 1, 0)),
@@ -310,26 +326,15 @@
         compiler_params=limit,
     )(live_count, destination, cell_index, particles, pair_order, accepted, direction, up)
     arrived = from_behind(theirs, "rep", 1)
-    from_upper = from_behind(movers(-1, mine), "space", -1)
-
     moved, samples = pl.pallas_call(
-        functools.partial(above_kernel, parts),
-        in_specs=[ANY, whole((6, MOVE, PART)), whole((4, CELLS // 2)), whole((4, CELLS // 2))],
-        out_specs=[whole((6, 1, MOVE, PART)), whole((4, 1, CELLS // 2))],
+        functools.partial(arrivals_kernel, parts),
+        in_specs=[HBM, VMEM, VMEM, VMEM, VMEM],
+        out_specs=[HBM, VMEM],
         out_shape=[jax.ShapeDtypeStruct(moved.shape, f32), jax.ShapeDtypeStruct((4, 1, CELLS // 2), f32)],
         input_output_aliases={0: 0},
-        grid=(1,),
+        scratch_shapes=[pltpu.SemaphoreType.DMA((2,))],
         compiler_params=pltpu.CompilerParams(vmem_limit_bytes=8 * 2**20),
-    )(moved, from_lower, mine, arrived)
-    moved = pl.pallas_call(
-        below_kernel,
-        in_specs=[ANY, whole((6, MOVE, PART))],
-        out_specs=whole((6, 1, MOVE, PART), (0, 0, 5, 0)),
-        out_shape=jax.ShapeDtypeStruct(moved.shape, f32),
-        input_output_aliases={0: 0},
-        grid=(1,),
-        compiler_params=pltpu.CompilerParams(vmem_limit_bytes=8 * 2**20),
-    )(moved, from_upper)
+    )(moved, from_lower, from_upper, mine, arrived)
     return (moved, samples)
 
 

time: 35.1 us -> 32 us (0.912)
  Pallas kernels: 16.7 us -> 13.2 us
  local copies, waits for them, and re-layouts: 0.01 us -> 0.68 us
  waiting for transfers between devices: 6.36 us -> 5.93 us
    pallas_call x4 -> x2, Pallas kernels: 9.04 us -> 5.46 us  [the longest x1 3.99 us: per_device(): pl.pallas_call(movers_kernel, in_specs=[HBM] * 5, out_specs=[VMEM, VMEM],...]
    unnamed x4 -> x2, local copies, waits for them, and re-layouts: 0.01 us -> 0.68 us
    ppermute x3, waiting for transfers between devices: 6.36 us -> 5.93 us  [from_behind(): return lax.ppermute(value, axis, pairs)]
  transfers between devices with their start and end apart: 3 -> 3, of which waited for: 2 -> 2; matrix products, arithmetic and copies ran while one was open for 0% -> 0% of each run, Pallas kernels for 35% -> 25%
where the time goes in v3:
time: 32 us; the launch traced here: 31.4 us
  Pallas kernels  13.2 us (41%)
  starting transfers between devices  10.3 us (32%)
  waiting for transfers between devices  5.93 us (19%)
  between operations  1.29 us (4%)
  local copies, waits for them, and re-layouts  0.68 us (2%)
    ppermute x3, starting transfers between devices, from_behind(): return lax.ppermute(value, axis, pairs)  10.3 us
    pallas_call x1, Pallas kernels, per_device(): pl.pallas_call(own_kernel, grid=(CAP // PART,), in_specs=[SMEM, lanes, la...  7.71 us
    ppermute x3, waiting for transfers between devices, from_behind(): return lax.ppermute(value, axis, pairs)  5.93 us
    pallas_call x1, Pallas kernels, per_device(): pl.pallas_call(movers_kernel, in_specs=[HBM] * 5, out_specs=[VMEM, VMEM],...  3.99 us
    pallas_call x1, Pallas kernels, per_device(): pl.pallas_call(functools.partial(arrivals_kernel, parts), in_specs=[HBM,...  1.47 us
    unnamed x2, local copies, waits for them, and re-layouts  0.68 us
  transfers between devices with their start and end apart: 3, of which 2 were waited for; matrix products, arithmetic and copies ran while one was open for 0% of the time, Pallas kernels for 25%

profile of v3, /device:TPU:1, one launch (start us, length us, event | category | flops | bytes accessed | tf_op | source)
XLA Modules:
  0.0 31.4 jit_solution(16615079618140097958)
XLA Ops:
  0.6 4.0 %shard_map.86 = (f32[6,128,128]{2,1,0:T(8,128)}, f32[6,128,128]{2,1,0:T(8,128)}) custom-call(s32[1,512]{1,0:T(1,128)} %destination.3, s32[1,512,128]{2,1,0:T(8,128)} %order.3, s32[1,64,512]{2,1,0:T(8,128)} %bitcast.2, s32[1,64,512]{2,1,0:T(8,128)} %bitcast.4, f32[6,1,512,128]{3,2,1,0:T(8,128)} %particles.3), custom_call_target="tpu_custom_call" | custom-call | tf_op jit(solution)/shard_map/pallas_call | solution.py:285
  4.6 9.3 %collective-permute-start.1 = (f32[6,128,128]{2,1,0:T(8,128)}, f32[6,128,128]{2,1,0:T(8,128)S(1)}, u32[]{:S(2)}, u32[]{:S(2)}) collective-permute-start(f32[6,128,128]{2,1,0:T(8,128)} %get-tuple-element.9), channel_id=1, source_target_pairs={{0,63},{1,0},{2,1},{3,2},{4,3},{5,4},{6,5},{7,6},{8,7},{9,8},{10,9... | collective-permute-start | bytes 1179656 | tf_op jit(solution)/shard_map/ppermute | solution.py:274
  13.9 0.0 collective-permute-start
  14.6 7.7 %shard_map.87 = (f32[6,1,768,128]{3,2,1,0:T(8,128)}, f32[4,128]{1,0:T(4,128)}, f32[4,128]{1,0:T(4,128)}) custom-call(s32[1,1]{1,0:T(1,128)S(6)} %copy.11.live_count, s32[1,512]{1,0:T(1,128)} %destination.3, s32[1,512]{1,0:T(1,128)} %cells.1, f32[6,1,512,128]{3,2,1,0:T(8,128)} %particles.3, s32[1,512,128]{2,1,0:T(8,128)} %order.3, s32[1,64,512]{2,1,0:T(8,128)} %bitcast.3, ...), custom_call_target="tpu_custom_call" | custom-call | tf_op jit(solution)/shard_map/pallas_call | solution.py:306
  22.3 1.0 %collective-permute-start.2 = (f32[4,128]{1,0:T(4,128)}, f32[4,128]{1,0:T(4,128)S(1)}, u32[]{:S(2)}, u32[]{:S(2)}) collective-permute-start(f32[4,128]{1,0:T(4,128)} %get-tuple-element.11), channel_id=1, source_target_pairs={{0,64},{64,0},{1,65},{65,1},{2,66},{66,2},{3,67},{67,3},{4,68},{68... | collective-permute-start | bytes 6152 | tf_op jit(solution)/shard_map/ppermute | solution.py:274
  23.3 1.0 %collective-permute-done.2.arrived = f32[4,128]{1,0:T(4,128)S(1)} collective-permute-done((f32[4,128]{1,0:T(4,128)}, f32[4,128]{1,0:T(4,128)S(1)}, u32[]{:S(2)}, u32[]{:S(2)}) %collective-permute-start.2) | collective-permute-done | bytes 2080 | tf_op jit(solution)/shard_map/ppermute | solution.py:274
  24.3 0.0 collective-permute-done.1.above
  24.3 4.9 %collective-permute-done.below = f32[6,128,128]{2,1,0:T(8,128)S(1)} collective-permute-done((f32[6,128,128]{2,1,0:T(8,128)}, f32[6,128,128]{2,1,0:T(8,128)S(1)}, u32[]{:S(2)}, u32[]{:S(2)}) %collective-permute-start) | collective-permute-done | bytes 393248 | tf_op jit(solution)/shard_map/ppermute | solution.py:274
  29.2 0.0 copy-start
  29.2 0.7 %copy-done = f32[4,128]{1,0:T(4,128)S(1)} copy-done((f32[4,128]{1,0:T(4,128)S(1)}, f32[4,128]{1,0:T(4,128)}, u32[]{:S(2)}) %copy-start) | copy-done | bytes 2072
  29.9 1.5 %shard_map.88 = (f32[6,1,768,128]{3,2,1,0:T(8,128)}, f32[4,1,128]{2,1,0:T(1,128)}) custom-call(f32[6,1,768,128]{3,2,1,0:T(8,128)} %get-tuple-element.8.held, f32[6,128,128]{2,1,0:T(8,128)S(1)} %collective-permute-done.below, f32[6,128,128]{2,1,0:T(8,128)S(1)} %collective-permute-done.1.above, f32[4,128]{1,0:T(4,128)S(1)} %copy-done, ...), custom_call_target="tpu_custom_call", output_to_operand_aliasing={{0}: (0, {})} | custom-call | tf_op jit(solution)/shard_map/pallas_call | solution.py:329
Async XLA Ops:
  4.6 19.7 %collective-permute-start.1 = (f32[6,128,128]{2,1,0:T(8,128)}, f32[6,128,128]{2,1,0:T(8,128)S(1)}, u32[]{:S(2)}, u32[]{:S(2)}) collective-permute-start(f32[6,128,128]{2,1,0:T(8,128)} %get-tuple-element.9), channel_id=1, source_target_pairs={{0,63},{1,0},{2,1},{3,2},{4,3},{5,4},{6,5},{7,6},{8,7},{9,8},{10,9... | collective-permute-start | bytes 1179656 | tf_op jit(solution)/shard_map/ppermute | solution.py:274
  13.9 15.3 %collective-permute-start = (f32[6,128,128]{2,1,0:T(8,128)}, f32[6,128,128]{2,1,0:T(8,128)S(1)}, u32[]{:S(2)}, u32[]{:S(2)}) collective-permute-start(f32[6,128,128]{2,1,0:T(8,128)} %get-tuple-element.7.sent), channel_id=1, source_target_pairs={{0,1},{1,2},{2,3},{3,4},{4,5},{5,6},{6,7},{7,8},{8,9},{9,10},{10,1... | collective-permute-start | bytes 1179656 | tf_op jit(solution)/shard_map/ppermute | solution.py:274
  22.3 2.0 %collective-permute-start.2 = (f32[4,128]{1,0:T(4,128)}, f32[4,128]{1,0:T(4,128)S(1)}, u32[]{:S(2)}, u32[]{:S(2)}) collective-permute-start(f32[4,128]{1,0:T(4,128)} %get-tuple-element.11), channel_id=1, source_target_pairs={{0,64},{64,0},{1,65},{65,1},{2,66},{66,2},{3,67},{67,3},{4,68},{68... | collective-permute-start | bytes 6152 | tf_op jit(solution)/shard_map/ppermute | solution.py:274
  29.2 0.7 %copy-start = (f32[4,128]{1,0:T(4,128)S(1)}, f32[4,128]{1,0:T(4,128)}, u32[]{:S(2)}) copy-start(f32[4,128]{1,0:T(4,128)} %get-tuple-element.10.mine) | copy-start | bytes 6148

commit v4 on v3

--- a/solution.py
+++ b/solution.py
@@ -224,36 +224,40 @@
     onehot = lax.broadcasted_iota(jnp.int32, (CELLS, PART), 0) == cell
     onehot = jnp.where(onehot, 1.0, 0.0).astype(jnp.bfloat16)
     squares = result[0] * result[0] + result[1] * result[1] + result[2] * result[2]
-    for c, value in enumerate([*result, squares]):
-        part = pick(onehot, value)
-
-        @pl.when(step == 0)
-        def _():
-            total[c] = part
-
-        @pl.when(step > 0)
-        def _():
-            total[c] += part
+    ones = jnp.ones((8, PART), jnp.bfloat16)
+    sums = []
+    for value in [*result, squares]:
+        high, low = split(value)
+        sums.append((dot_lanes(ones, high) + dot_lanes(ones, low))[:1])
+    high, low = split(jnp.concatenate(sums + [jnp.zeros((4, PART), jnp.float32)], axis=0))
+    part = dot_lanes(high, onehot) + dot_lanes(low, onehot)
+
+    @pl.when(step == 0)
+    def _():
+        total[...] = part
+
+    @pl.when(step > 0)
+    def _():
+        total[...] += part
 
     @pl.when(step == CAP // PART - 1)
     def _():
-        ones = jnp.ones((8, PART), jnp.bfloat16)
-        for c in range(4):
-            high, low = split(total[c])
-            sums = dot_lanes(ones, high) + dot_lanes(ones, low)
-            mine[c : c + 1] = sums[:1, : CELLS // 2]
-            theirs[c : c + 1] = sums[:1, CELLS // 2 :]
-
-
-def arrivals_kernel(parts, held, below, above, mine, arrived, moved, samples, sems):
-    del held
+        mine[...] = total[:4, : CELLS // 2]
+        theirs[...] = total[:4, CELLS // 2 :]
+
+
+def samples_kernel(parts, mine, arrived, samples):
+    samples[:, 0] = (mine[...] + arrived[...]) * (1.0 / (PART * parts))
+
+
+def arrivals_kernel(held, ready, below, above, moved, samples, sems):
+    del held, ready, samples
     copies = [
         pltpu.make_async_copy(below, moved.at[:, 0, 0:MOVE], sems.at[0]),
         pltpu.make_async_copy(above, moved.at[:, 0, MOVE + CAP : OUTCAP], sems.at[1]),
     ]
     for c in copies:
         c.start()
-    samples[:, 0] = (mine[...] + arrived[...]) * (1.0 / (PART * parts))
     for c in copies:
         c.wait()
 
@@ -322,19 +326,27 @@
             whole((4, CELLS // 2)),
         ],
         out_shape=[jax.ShapeDtypeStruct((6, 1, OUTCAP, PART), f32), half, half],
-        scratch_shapes=[pltpu.VMEM((4, CELLS, PART), f32)],
+        scratch_shapes=[pltpu.VMEM((8, CELLS), f32)],
         compiler_params=limit,
-    )(live_count, destination, cell_index, particles, pair_order, accepted, direction, up)
+    )(live_count, destination, cell_index, particles, pair_order, accepted, direction, down)
     arrived = from_behind(theirs, "rep", 1)
+    small = pltpu.CompilerParams(vmem_limit_bytes=8 * 2**20)
+    samples = pl.pallas_call(
+        functools.partial(samples_kernel, parts),
+        in_specs=[VMEM, VMEM],
+        out_specs=VMEM,
+        out_shape=jax.ShapeDtypeStruct((4, 1, CELLS // 2), f32),
+        compiler_params=small,
+    )(mine, arrived)
     moved, samples = pl.pallas_call(
-        functools.partial(arrivals_kernel, parts),
-        in_specs=[HBM, VMEM, VMEM, VMEM, VMEM],
-        out_specs=[HBM, VMEM],
-        out_shape=[jax.ShapeDtypeStruct(moved.shape, f32), jax.ShapeDtypeStruct((4, 1, CELLS // 2), f32)],
-        input_output_aliases={0: 0},
+        arrivals_kernel,
+        in_specs=[HBM, HBM, VMEM, VMEM],
+        out_specs=[HBM, HBM],
+        out_shape=[jax.ShapeDtypeStruct(moved.shape, f32), jax.ShapeDtypeStruct(samples.shape, f32)],
+        input_output_aliases={0: 0, 1: 1},
         scratch_shapes=[pltpu.SemaphoreType.DMA((2,))],
-        compiler_params=pltpu.CompilerParams(vmem_limit_bytes=8 * 2**20),
-    )(moved, from_lower, from_upper, mine, arrived)
+        compiler_params=small,
+    )(moved, samples, from_lower, from_upper)
     return (moved, samples)
 
 

time: 32 us -> 25 us (0.78); the launches traced: 31.4 us -> 24.8 us
  waiting for transfers between devices: 5.93 us -> 1.04 us
  Pallas kernels: 13.2 us -> 11.4 us
    ppermute x3, waiting for transfers between devices: 5.93 us -> 1.04 us  [from_behind(): return lax.ppermute(value, axis, pairs)]
    pallas_call x1, Pallas kernels: 7.71 us -> 5.9 us  [per_device(): pl.pallas_call(own_kernel, grid=(CAP // PART,), in_specs=[SMEM, lanes, la...]
    pallas_call x1 -> x2, Pallas kernels: 1.47 us -> 1.48 us  [the longest x1 0.89 us: per_device(): pl.pallas_call(arrivals_kernel, in_specs=[HBM, HBM, VMEM, VMEM], out_spec...]
  transfers between devices with their start and end apart: 3 -> 3, of which waited for: 2 -> 1; matrix products, arithmetic and copies ran while one was open for 0% -> 0% of each run, Pallas kernels for 25% -> 26%
where the time goes in v4:
time: 25 us; the launch traced here: 24.8 us
  Pallas kernels  11.4 us (46%)
  starting transfers between devices  10.4 us (42%)
  between operations  1.29 us (5%)
  waiting for transfers between devices  1.04 us (4%)
  local copies, waits for them, and re-layouts  0.68 us (3%)
    ppermute x3, starting transfers between devices, from_behind(): return lax.ppermute(value, axis, pairs)  10.4 us
    pallas_call x1, Pallas kernels, per_device(): pl.pallas_call(own_kernel, grid=(CAP // PART,), in_specs=[SMEM, lanes, la...  5.9 us
    pallas_call x1, Pallas kernels, per_device(): pl.pallas_call(movers_kernel, in_specs=[HBM] * 5, out_specs=[VMEM, VMEM],...  3.99 us
    ppermute x3, waiting for transfers between devices, from_behind(): return lax.ppermute(value, axis, pairs)  1.04 us
    pallas_call x1, Pallas kernels, per_device(): pl.pallas_call(arrivals_kernel, in_specs=[HBM, HBM, VMEM, VMEM], out_spec...  0.89 us
    unnamed x2, local copies, waits for them, and re-layouts  0.68 us
    pallas_call x1, Pallas kernels, per_device(): pl.pallas_call(functools.partial(samples_kernel, parts), in_specs=[VMEM,...  0.59 us
  transfers between devices with their start and end apart: 3, of which 1 were waited for; matrix products, arithmetic and copies ran while one was open for 0% of the time, Pallas kernels for 26%

profile of v4, /device:TPU:1, one launch (start us, length us, event | category | flops | bytes accessed | tf_op | source)
XLA Modules:
  0.0 24.8 jit_solution(2662747265488388626)
XLA Ops:
  0.6 4.0 %shard_map.86 = (f32[6,128,128]{2,1,0:T(8,128)}, f32[6,128,128]{2,1,0:T(8,128)}) custom-call(s32[1,512]{1,0:T(1,128)} %destination.3, s32[1,512,128]{2,1,0:T(8,128)} %order.3, s32[1,64,512]{2,1,0:T(8,128)} %bitcast.2, s32[1,64,512]{2,1,0:T(8,128)} %bitcast.4, f32[6,1,512,128]{3,2,1,0:T(8,128)} %particles.3), custom_call_target="tpu_custom_call" | custom-call | tf_op jit(solution)/shard_map/pallas_call | solution.py:289
  4.6 2.1 %collective-permute-start.1 = (f32[6,128,128]{2,1,0:T(8,128)}, f32[6,128,128]{2,1,0:T(8,128)S(1)}, u32[]{:S(2)}, u32[]{:S(2)}) collective-permute-start(f32[6,128,128]{2,1,0:T(8,128)} %get-tuple-element.11), channel_id=1, source_target_pairs={{0,1},{1,2},{2,3},{3,4},{4,5},{5,6},{6,7},{7,8},{8,9},{9,10},{10,1... | collective-permute-start | bytes 1179656 | tf_op jit(solution)/shard_map/ppermute | solution.py:278
  6.7 7.3 %collective-permute-start.2 = (f32[6,128,128]{2,1,0:T(8,128)}, f32[6,128,128]{2,1,0:T(8,128)S(1)}, u32[]{:S(2)}, u32[]{:S(2)}) collective-permute-start(f32[6,128,128]{2,1,0:T(8,128)} %get-tuple-element.7.sent), channel_id=1, source_target_pairs={{0,63},{1,0},{2,1},{3,2},{4,3},{5,4},{6,5},{7,6},{8,7},{9,8},{10,9... | collective-permute-start | bytes 1179656 | tf_op jit(solution)/shard_map/ppermute | solution.py:278
  14.7 5.9 %shard_map.87 = (f32[6,1,768,128]{3,2,1,0:T(8,128)}, f32[4,128]{1,0:T(4,128)}, f32[4,128]{1,0:T(4,128)}) custom-call(s32[1,1]{1,0:T(1,128)S(6)} %copy.13.live_count, s32[1,512]{1,0:T(1,128)} %destination.3, s32[1,512]{1,0:T(1,128)} %cells.1, f32[6,1,512,128]{3,2,1,0:T(8,128)} %particles.3, s32[1,512,128]{2,1,0:T(8,128)} %order.3, s32[1,64,512]{2,1,0:T(8,128)} %bitcast.3, ...), custom_call_target="tpu_custom_call" | custom-call | tf_op jit(solution)/shard_map/pallas_call | solution.py:310
  20.6 1.0 %collective-permute-start = (f32[4,128]{1,0:T(4,128)}, f32[4,128]{1,0:T(4,128)S(1)}, u32[]{:S(2)}, u32[]{:S(2)}) collective-permute-start(f32[4,128]{1,0:T(4,128)} %get-tuple-element.10), channel_id=1, source_target_pairs={{0,64},{64,0},{1,65},{65,1},{2,66},{66,2},{3,67},{67,3},{4,68},{68... | collective-permute-start | bytes 6152 | tf_op jit(solution)/shard_map/ppermute | solution.py:278
  21.6 1.0 %collective-permute-done.arrived = f32[4,128]{1,0:T(4,128)S(1)} collective-permute-done((f32[4,128]{1,0:T(4,128)}, f32[4,128]{1,0:T(4,128)S(1)}, u32[]{:S(2)}, u32[]{:S(2)}) %collective-permute-start) | collective-permute-done | bytes 2080 | tf_op jit(solution)/shard_map/ppermute | solution.py:278
  22.6 0.0 copy-start
  22.6 0.7 %copy-done = f32[4,128]{1,0:T(4,128)S(1)} copy-done((f32[4,128]{1,0:T(4,128)S(1)}, f32[4,128]{1,0:T(4,128)}, u32[]{:S(2)}) %copy-start) | copy-done | bytes 2072
  23.3 0.6 %shard_map.88.ready = f32[4,1,128]{2,1,0:T(1,128)} custom-call(f32[4,128]{1,0:T(4,128)S(1)} %copy-done, f32[4,128]{1,0:T(4,128)S(1)} %collective-permute-done.arrived), custom_call_target="tpu_custom_call" | custom-call | tf_op jit(solution)/shard_map/pallas_call | solution.py:334
  23.9 0.0 collective-permute-done.1.below
  23.9 0.0 collective-permute-done.2.above
  23.9 0.9 %shard_map.89 = (f32[6,1,768,128]{3,2,1,0:T(8,128)}, f32[4,1,128]{2,1,0:T(1,128)}) custom-call(f32[6,1,768,128]{3,2,1,0:T(8,128)} %get-tuple-element.8.held, f32[4,1,128]{2,1,0:T(1,128)} %shard_map.88.ready, f32[6,128,128]{2,1,0:T(8,128)S(1)} %collective-permute-done.1.below, ...), custom_call_target="tpu_custom_call", output_to_operand_aliasing={{0}: (0, {}), {1}: (1, {})} | custom-call | tf_op jit(solution)/shard_map/pallas_call | solution.py:341
Async XLA Ops:
  4.6 19.3 %collective-permute-start.1 = (f32[6,128,128]{2,1,0:T(8,128)}, f32[6,128,128]{2,1,0:T(8,128)S(1)}, u32[]{:S(2)}, u32[]{:S(2)}) collective-permute-start(f32[6,128,128]{2,1,0:T(8,128)} %get-tuple-element.11), channel_id=1, source_target_pairs={{0,1},{1,2},{2,3},{3,4},{4,5},{5,6},{6,7},{7,8},{8,9},{9,10},{10,1... | collective-permute-start | bytes 1179656 | tf_op jit(solution)/shard_map/ppermute | solution.py:278
  6.7 17.1 %collective-permute-start.2 = (f32[6,128,128]{2,1,0:T(8,128)}, f32[6,128,128]{2,1,0:T(8,128)S(1)}, u32[]{:S(2)}, u32[]{:S(2)}) collective-permute-start(f32[6,128,128]{2,1,0:T(8,128)} %get-tuple-element.7.sent), channel_id=1, source_target_pairs={{0,63},{1,0},{2,1},{3,2},{4,3},{5,4},{6,5},{7,6},{8,7},{9,8},{10,9... | collective-permute-start | bytes 1179656 | tf_op jit(solution)/shard_map/ppermute | solution.py:278
  20.6 2.0 %collective-permute-start = (f32[4,128]{1,0:T(4,128)}, f32[4,128]{1,0:T(4,128)S(1)}, u32[]{:S(2)}, u32[]{:S(2)}) collective-permute-start(f32[4,128]{1,0:T(4,128)} %get-tuple-element.10), channel_id=1, source_target_pairs={{0,64},{64,0},{1,65},{65,1},{2,66},{66,2},{3,67},{67,3},{4,68},{68... | collective-permute-start | bytes 6152 | tf_op jit(solution)/shard_map/ppermute | solution.py:278
  22.6 0.7 %copy-start = (f32[4,128]{1,0:T(4,128)S(1)}, f32[4,128]{1,0:T(4,128)}, u32[]{:S(2)}) copy-start(f32[4,128]{1,0:T(4,128)} %get-tuple-element.9.mine) | copy-start | bytes 6148

commit v5 on v3

--- a/solution.py
+++ b/solution.py
@@ -164,7 +164,7 @@
 
 
 def movers_kernel(
-    destination, order, accepted, direction, particles, up, down, targets, orders, takens, turns, data, sems
+    destination, order, accepted, direction, particles, cell, up, down, targets, orders, takens, turns, data, cells, sems
 ):
     copies = [
         pltpu.make_async_copy(source, target, sems.at[i])
@@ -176,6 +176,7 @@
                 (direction, turns),
                 (particles.at[3:6], data.at[3:6]),
                 (particles.at[0:3], data.at[0:3]),
+                (cell, cells),
             )
         )
     ]
@@ -202,58 +203,59 @@
         for c in range(3):
             out[3 + c] = result[c]
             out[c] = position[c][part] + time_step * result[c]
-
-
-def own_kernel(live_count, destination, cells, particles, order, accepted, direction, sent, moved, mine, theirs, total):
-    del sent
-    step = pl.program_id(0)
-    slots = lax.broadcasted_iota(jnp.int32, (1, PART), 1) + step * PART
+    copies[6].wait()
+
+
+def own_kernel(live_count, destination, order, accepted, direction, particles, cells, moved, mine, theirs, out, sems):
     slab, rep = place_on_mesh()
-    live = slots < live_count[0, 0]
-    staying = jnp.where(live & (destination[...] == slab), 1.0, 0.0)
-    info = jnp.where(accepted[0] == 1, direction[0], -1).astype(jnp.float32)
-    codes = partner_codes(order[0].astype(jnp.float32).T, info) + staying * 8388608.0
-    codes = codes.T.astype(jnp.int32)
-    keep = (codes >> 23) == 1
-    result = collide([particles[3 + c, 0] for c in range(3)], codes)
-    for c in range(3):
-        moved[3 + c, 0] = jnp.where(keep, result[c], 0.0)
-        moved[c, 0] = jnp.where(keep, particles[c, 0] + time_step * result[c], 0.0)
-    cell = (cells[...] + rep * (CELLS // 2)) & (CELLS - 1)
-    cell = jnp.where(live, cell, -1)
-    onehot = lax.broadcasted_iota(jnp.int32, (CELLS, PART), 0) == cell
-    onehot = jnp.where(onehot, 1.0, 0.0).astype(jnp.bfloat16)
-    squares = result[0] * result[0] + result[1] * result[1] + result[2] * result[2]
-    for c, value in enumerate([*result, squares]):
-        part = pick(onehot, value)
-
-        @pl.when(step == 0)
-        def _():
-            total[c] = part
-
-        @pl.when(step > 0)
-        def _():
-            total[c] += part
-
-    @pl.when(step == CAP // PART - 1)
-    def _():
-        ones = jnp.ones((8, PART), jnp.bfloat16)
-        for c in range(4):
-            high, low = split(total[c])
-            sums = dot_lanes(ones, high) + dot_lanes(ones, low)
-            mine[c : c + 1] = sums[:1, : CELLS // 2]
-            theirs[c : c + 1] = sums[:1, CELLS // 2 :]
-
-
-def arrivals_kernel(parts, held, below, above, mine, arrived, moved, samples, sems):
+    live = lax.broadcasted_iota(jnp.int32, (1, CAP), 1) < live_count[0, 0]
+    staying = jnp.where(live & (destination[...] == slab), 8388608.0, 0.0)
+    cell = jnp.where(live, (cells[...] + rep * (CELLS // 2)) & (CELLS - 1), -1)
+    ones = jnp.ones((8, PART), jnp.bfloat16)
+    total = jnp.zeros((8, CELLS), jnp.float32)
+    copies = []
+    for i in range(CAP // PART):
+        part = slice(i * PART, (i + 1) * PART)
+        info = jnp.where(accepted[0, :, part] == 1, direction[0, :, part], -1).astype(jnp.float32)
+        codes = partner_codes(order[0, part].astype(jnp.float32).T, info) + staying[:, part]
+        codes = codes.T.astype(jnp.int32)
+        keep = (codes >> 23) == 1
+        result = collide([particles[3 + c, 0, part] for c in range(3)], codes)
+        for c in range(3):
+            out[3 + c, part] = jnp.where(keep, result[c], 0.0)
+            out[c, part] = jnp.where(keep, particles[c, 0, part] + time_step * result[c], 0.0)
+        copies.append(
+            pltpu.make_async_copy(
+                out.at[:, part], moved.at[:, 0, MOVE + i * PART : MOVE + (i + 1) * PART], sems.at[i]
+            )
+        )
+        copies[i].start()
+        onehot = lax.broadcasted_iota(jnp.int32, (CELLS, PART), 0) == cell[:, part]
+        onehot = jnp.where(onehot, 1.0, 0.0).astype(jnp.bfloat16)
+        squares = result[0] * result[0] + result[1] * result[1] + result[2] * result[2]
+        sums = []
+        for value in [*result, squares]:
+            high, low = split(value)
+            sums.append((dot_lanes(ones, high) + dot_lanes(ones, low))[:1])
+        high, low = split(jnp.concatenate(sums + [jnp.zeros((4, PART), jnp.float32)], axis=0))
+        total += dot_lanes(high, onehot) + dot_lanes(low, onehot)
+    mine[...] = total[:4, : CELLS // 2]
+    theirs[...] = total[:4, CELLS // 2 :]
+    for c in copies:
+        c.wait()
+
+
+def arrivals_kernel(parts, held, below, above, mine, arrived, moved, samples, sums, sems):
     del held
     copies = [
         pltpu.make_async_copy(below, moved.at[:, 0, 0:MOVE], sems.at[0]),
         pltpu.make_async_copy(above, moved.at[:, 0, MOVE + CAP : OUTCAP], sems.at[1]),
+        pltpu.make_async_copy(sums, samples, sems.at[2]),
     ]
-    for c in copies:
-        c.start()
-    samples[:, 0] = (mine[...] + arrived[...]) * (1.0 / (PART * parts))
+    copies[0].start()
+    copies[1].start()
+    sums[:, 0] = (mine[...] + arrived[...]) * (1.0 / (PART * parts))
+    copies[2].start()
     for c in copies:
         c.wait()
 
@@ -266,6 +268,10 @@
 SMEM = pl.BlockSpec(memory_space=pltpu.SMEM)
 VMEM = pl.BlockSpec(memory_space=pltpu.VMEM)
 HBM = pl.BlockSpec(memory_space=pltpu.HBM)
+
+
+def in_hbm(*arrays):
+    return [pltpu.with_memory_space_constraint(a, pltpu.HBM) for a in arrays]
 
 
 def from_behind(value, axis, steps):
@@ -279,60 +285,46 @@
     direction = jnp.swapaxes(direction, 1, 2)
     parts = lax.axis_size("rep")
     f32 = jnp.float32
-    limit = pltpu.CompilerParams(vmem_limit_bytes=56 * 2**20)
+    limit = pltpu.CompilerParams(vmem_limit_bytes=32 * 2**20)
 
     sent = jax.ShapeDtypeStruct((6, MOVE, PART), f32)
-    up, down = pl.pallas_call(
+    up, down, *held = pl.pallas_call(
         movers_kernel,
-        in_specs=[HBM] * 5,
-        out_specs=[VMEM, VMEM],
-        out_shape=[sent, sent],
-        scratch_shapes=[
+        in_specs=[HBM] * 6,
+        out_specs=[VMEM] * 8,
+        out_shape=[
+            sent,
+            sent,
             pltpu.VMEM((1, CAP), jnp.int32),
             pltpu.VMEM((1, CAP, PART), jnp.int32),
             pltpu.VMEM((1, PAIRS, CAP), jnp.int32),
             pltpu.VMEM((1, PAIRS, CAP), jnp.int32),
             pltpu.VMEM((6, 1, CAP, PART), f32),
-            pltpu.SemaphoreType.DMA((6,)),
+            pltpu.VMEM((1, CAP), jnp.int32),
         ],
+        scratch_shapes=[pltpu.SemaphoreType.DMA((7,))],
         compiler_params=limit,
-    )(destination, pair_order, accepted, direction, particles)
+    )(*in_hbm(destination, pair_order, accepted, direction, particles, cell_index))
     from_lower = from_behind(up, "space", 1)
     from_upper = from_behind(down, "space", -1)
 
-    lanes = pl.BlockSpec((1, PART), lambda i: (0, i))
-    pairs = pl.BlockSpec((1, PAIRS, PART), lambda i: (0, 0, i))
     half = jax.ShapeDtypeStruct((4, CELLS // 2), f32)
     moved, mine, theirs = pl.pallas_call(
         own_kernel,
-        grid=(CAP // PART,),
-        in_specs=[
-            SMEM,
-            lanes,
-            lanes,
-            pl.BlockSpec((6, 1, PART, PART), lambda i: (0, 0, i, 0)),
-            pl.BlockSpec((1, PART, PART), lambda i: (0, i, 0)),
-            pairs,
-            pairs,
-            HBM,
-        ],
-        out_specs=[
-            pl.BlockSpec((6, 1, PART, PART), lambda i: (0, 0, i + 1, 0)),
-            whole((4, CELLS // 2)),
-            whole((4, CELLS // 2)),
-        ],
+        in_specs=[SMEM] + [VMEM] * 6,
+        out_specs=[HBM, VMEM, VMEM],
         out_shape=[jax.ShapeDtypeStruct((6, 1, OUTCAP, PART), f32), half, half],
-        scratch_shapes=[pltpu.VMEM((4, CELLS, PART), f32)],
+        scratch_shapes=[pltpu.VMEM((6, CAP, PART), f32), pltpu.SemaphoreType.DMA((CAP // PART,))],
         compiler_params=limit,
-    )(live_count, destination, cell_index, particles, pair_order, accepted, direction, up)
+    )(live_count, *held)
     arrived = from_behind(theirs, "rep", 1)
     moved, samples = pl.pallas_call(
         functools.partial(arrivals_kernel, parts),
         in_specs=[HBM, VMEM, VMEM, VMEM, VMEM],
-        out_specs=[HBM, VMEM],
+        out_specs=[HBM, HBM],
         out_shape=[jax.ShapeDtypeStruct(moved.shape, f32), jax.ShapeDtypeStruct((4, 1, CELLS // 2), f32)],
         input_output_aliases={0: 0},
-        scratch_shapes=[pltpu.SemaphoreType.DMA((2,))],
+        scratch_shapes=[pltpu.VMEM((4, 1, CELLS // 2), f32), pltpu.SemaphoreType.DMA((3,))],
         compiler_params=pltpu.CompilerParams(vmem_limit_bytes=8 * 2**20),
     )(moved, from_lower, from_upper, mine, arrived)
     return (moved, samples)

time: 32 us -> 23 us (0.72); the launches traced: 31.4 us -> 22.8 us
  Pallas kernels: 13.2 us -> 6.86 us
  waiting for transfers between devices: 5.93 us -> 4.25 us
  local copies, waits for them, and re-layouts: 0.68 us -> 0 us
    pallas_call x2, Pallas kernels: 11.7 us -> 5.95 us  [the longest x1 3.13 us: per_device(): pl.pallas_call(movers_kernel, in_specs=[HBM] * 6, out_specs=[VMEM] * 8, o...]
    ppermute x3, waiting for transfers between devices: 5.93 us -> 4.25 us  [from_behind(): return lax.ppermute(value, axis, pairs)]
    unnamed x2 -> x0, local copies, waits for them, and re-layouts: 0.68 us -> none
    pallas_call x1, Pallas kernels: 1.47 us -> 0.9 us  [per_device(): pl.pallas_call(functools.partial(arrivals_kernel, parts), in_specs=[HBM,...]
  transfers between devices with their start and end apart: 3 -> 3, of which waited for: 2 -> 2; matrix products, arithmetic and copies ran while one was open for 0% -> 0% of each run, Pallas kernels for 25% -> 12%
where the time goes in v5:
time: 23 us; the launch traced here: 22.8 us
  starting transfers between devices  10.4 us (45%)
  Pallas kernels  6.86 us (30%)
  waiting for transfers between devices  4.25 us (18%)
  between operations  1.3 us (6%)
    ppermute x3, starting transfers between devices, from_behind(): return lax.ppermute(value, axis, pairs)  10.4 us
    ppermute x3, waiting for transfers between devices, from_behind(): return lax.ppermute(value, axis, pairs)  4.25 us
    pallas_call x1, Pallas kernels, per_device(): pl.pallas_call(movers_kernel, in_specs=[HBM] * 6, out_specs=[VMEM] * 8, o...  3.13 us
    pallas_call x1, Pallas kernels, per_device(): pl.pallas_call(own_kernel, in_specs=[SMEM] + [VMEM] * 6, out_specs=[HBM,...  2.82 us
    pallas_call x1, Pallas kernels, per_device(): pl.pallas_call(functools.partial(arrivals_kernel, parts), in_specs=[HBM,...  0.9 us
  transfers between devices with their start and end apart: 3, of which 2 were waited for; matrix products, arithmetic and copies ran while one was open for 0% of the time, Pallas kernels for 12%

profile of v5, /device:TPU:1, one launch (start us, length us, event | category | flops | bytes accessed | tf_op | source)
XLA Modules:
  0.0 22.8 jit_solution(11449556577938897613)
XLA Ops:
  0.6 3.1 %shard_map.86 = (f32[6,128,128]{2,1,0:T(8,128)S(1)}, f32[6,128,128]{2,1,0:T(8,128)S(1)}, s32[1,512]{1,0:T(1,128)S(1)}, s32[1,512,128]{2,1,0:T(8,128)S(1)}, s32[1...) custom-call(s32[1,512]{1,0:T(1,128)} %destination.1, ...), custom_call_target="tpu_custom_call" | custom-call | tf_op jit(solution)/shard_map/pallas_call | solution.py:291
  3.8 2.1 %collective-permute-start = (f32[6,128,128]{2,1,0:T(8,128)S(1)}, f32[6,128,128]{2,1,0:T(8,128)S(1)}, u32[]{:S(2)}, u32[]{:S(2)}) collective-permute-start(f32[6,128,128]{2,1,0:T(8,128)S(1)} %get-tuple-element.20), channel_id=1, source_target_pairs={{0,1},{1,2},{2,3},{3,4},{4,5},{5,6},{6,7},{7,8},{8,9},{9,10},{10,1... | collective-permute-start | bytes 1179656 | tf_op jit(solution)/shard_map/ppermute | solution.py:280
  5.9 7.3 %collective-permute-start.1 = (f32[6,128,128]{2,1,0:T(8,128)S(1)}, f32[6,128,128]{2,1,0:T(8,128)S(1)}, u32[]{:S(2)}, u32[]{:S(2)}) collective-permute-start(f32[6,128,128]{2,1,0:T(8,128)S(1)} %get-tuple-element.21), channel_id=1, source_target_pairs={{0,63},{1,0},{2,1},{3,2},{4,3},{5,4},{6,5},{7,6},{8,7},{9,8},{10,9... | collective-permute-start | bytes 1179656 | tf_op jit(solution)/shard_map/ppermute | solution.py:280
  13.8 2.8 %shard_map.87 = (f32[6,1,768,128]{3,2,1,0:T(8,128)}, f32[4,128]{1,0:T(4,128)S(1)}, f32[4,128]{1,0:T(4,128)S(1)}) custom-call(s32[1,1]{1,0:T(1,128)S(6)} %copy.11.live_count, s32[1,512]{1,0:T(1,128)S(1)} %get-tuple-element.13.destination, s32[1,512,128]{2,1,0:T(8,128)S(1)} %get-tuple-element.14.order, s32[1,64,512]{2,1,0:T(8,128)S(1)} %get-tuple-element.15.accepted, ...), custom_call_target="tpu_custom_call" | custom-call | tf_op jit(solution)/shard_map/pallas_call | solution.py:312
  16.6 1.0 %collective-permute-start.2 = (f32[4,128]{1,0:T(4,128)S(1)}, f32[4,128]{1,0:T(4,128)S(1)}, u32[]{:S(2)}, u32[]{:S(2)}) collective-permute-start(f32[4,128]{1,0:T(4,128)S(1)} %get-tuple-element.23), channel_id=1, source_target_pairs={{0,64},{64,0},{1,65},{65,1},{2,66},{66,2},{3,67},{67,3},{4,68},{68... | collective-permute-start | bytes 6152 | tf_op jit(solution)/shard_map/ppermute | solution.py:280
  17.7 0.8 %collective-permute-done.2.arrived = f32[4,128]{1,0:T(4,128)S(1)} collective-permute-done((f32[4,128]{1,0:T(4,128)S(1)}, f32[4,128]{1,0:T(4,128)S(1)}, u32[]{:S(2)}, u32[]{:S(2)}) %collective-permute-start.2) | collective-permute-done | bytes 2080 | tf_op jit(solution)/shard_map/ppermute | solution.py:280
  18.5 3.4 %collective-permute-done.below = f32[6,128,128]{2,1,0:T(8,128)S(1)} collective-permute-done((f32[6,128,128]{2,1,0:T(8,128)S(1)}, f32[6,128,128]{2,1,0:T(8,128)S(1)}, u32[]{:S(2)}, u32[]{:S(2)}) %collective-permute-start) | collective-permute-done | bytes 393248 | tf_op jit(solution)/shard_map/ppermute | solution.py:280
  21.9 0.0 collective-permute-done.1.above
  21.9 0.9 %shard_map.88 = (f32[6,1,768,128]{3,2,1,0:T(8,128)}, f32[4,1,128]{2,1,0:T(1,128)}) custom-call(f32[6,1,768,128]{3,2,1,0:T(8,128)} %get-tuple-element.19.held, f32[6,128,128]{2,1,0:T(8,128)S(1)} %collective-permute-done.below, f32[6,128,128]{2,1,0:T(8,128)S(1)} %collective-permute-done.1.above, ...), custom_call_target="tpu_custom_call", output_to_operand_aliasing={{0}: (0, {})} | custom-call | tf_op jit(solution)/shard_map/pallas_call | solution.py:321
Async XLA Ops:
  3.8 18.1 %collective-permute-start = (f32[6,128,128]{2,1,0:T(8,128)S(1)}, f32[6,128,128]{2,1,0:T(8,128)S(1)}, u32[]{:S(2)}, u32[]{:S(2)}) collective-permute-start(f32[6,128,128]{2,1,0:T(8,128)S(1)} %get-tuple-element.20), channel_id=1, source_target_pairs={{0,1},{1,2},{2,3},{3,4},{4,5},{5,6},{6,7},{7,8},{8,9},{9,10},{10,1... | collective-permute-start | bytes 1179656 | tf_op jit(solution)/shard_map/ppermute | solution.py:280
  5.9 16.0 %collective-permute-start.1 = (f32[6,128,128]{2,1,0:T(8,128)S(1)}, f32[6,128,128]{2,1,0:T(8,128)S(1)}, u32[]{:S(2)}, u32[]{:S(2)}) collective-permute-start(f32[6,128,128]{2,1,0:T(8,128)S(1)} %get-tuple-element.21), channel_id=1, source_target_pairs={{0,63},{1,0},{2,1},{3,2},{4,3},{5,4},{6,5},{7,6},{8,7},{9,8},{10,9... | collective-permute-start | bytes 1179656 | tf_op jit(solution)/shard_map/ppermute | solution.py:280
  16.6 1.9 %collective-permute-start.2 = (f32[4,128]{1,0:T(4,128)S(1)}, f32[4,128]{1,0:T(4,128)S(1)}, u32[]{:S(2)}, u32[]{:S(2)}) collective-permute-start(f32[4,128]{1,0:T(4,128)S(1)} %get-tuple-element.23), channel_id=1, source_target_pairs={{0,64},{64,0},{1,65},{65,1},{2,66},{66,2},{3,67},{67,3},{4,68},{68... | collective-permute-start | bytes 6152 | tf_op jit(solution)/shard_map/ppermute | solution.py:280

commit v6 on v5

--- a/solution.py
+++ b/solution.py
@@ -163,19 +163,19 @@
     return lax.rem(slab + SLABS + steps, SLABS)
 
 
-def movers_kernel(
-    destination, order, accepted, direction, particles, cell, up, down, targets, orders, takens, turns, data, cells, sems
+def position_kernel(
+    destination, order, accepted, direction, particles, cell, up, down, selected, targets, orders, takens, turns, data, cells, sems
 ):
     copies = [
         pltpu.make_async_copy(source, target, sems.at[i])
         for i, (source, target) in enumerate(
             (
                 (destination, targets),
+                (particles.at[0:3], data.at[0:3]),
                 (order, orders),
                 (accepted, takens),
                 (direction, turns),
                 (particles.at[3:6], data.at[3:6]),
-                (particles.at[0:3], data.at[0:3]),
                 (cell, cells),
             )
         )
@@ -184,29 +184,32 @@
         c.start()
     copies[0].wait()
     selection = mover_selection(targets[...])
-    for c in copies[1:4]:
+    selected[...] = selection
+    copies[1].wait()
+    for c in range(3):
+        position = pick(selection, data[c, 0])
+        up[c] = position[:MOVE]
+        down[c] = position[MOVE:]
+    for c in copies[2:]:
         c.wait()
+
+
+def velocity_kernel(selected, orders, takens, turns, data, up, down):
+    selection = selected[...]
     info = jnp.where(takens[0] == 1, turns[0], -1).astype(jnp.float32).astype(jnp.bfloat16)
     chosen = dot_lanes(info, selection)
     order_rows = dot(selection, orders[0].astype(jnp.float32).astype(jnp.bfloat16))
-    codes = []
-    for i in range(2):
-        part = slice(i * MOVE, (i + 1) * MOVE)
-        codes.append(partner_codes(order_rows[part].T, chosen[:, part]).T.astype(jnp.int32))
-    copies[4].wait()
     velocity = [pick(selection, data[3 + c, 0]) for c in range(3)]
-    copies[5].wait()
-    position = [pick(selection, data[c, 0]) for c in range(3)]
     for i, out in enumerate((up, down)):
         part = slice(i * MOVE, (i + 1) * MOVE)
-        result = collide([v[part] for v in velocity], codes[i])
+        codes = partner_codes(order_rows[part].T, chosen[:, part]).T.astype(jnp.int32)
+        result = collide([v[part] for v in velocity], codes)
         for c in range(3):
-            out[3 + c] = result[c]
-            out[c] = position[c][part] + time_step * result[c]
-    copies[6].wait()
-
-
-def own_kernel(live_count, destination, order, accepted, direction, particles, cells, moved, mine, theirs, out, sems):
+            out[c] = result[c]
+
+
+def own_kernel(live_count, destination, order, accepted, direction, particles, cells, sent, moved, mine, theirs, out, sems):
+    del sent
     slab, rep = place_on_mesh()
     live = lax.broadcasted_iota(jnp.int32, (1, CAP), 1) < live_count[0, 0]
     staying = jnp.where(live & (destination[...] == slab), 8388608.0, 0.0)
@@ -245,17 +248,23 @@
         c.wait()
 
 
-def arrivals_kernel(parts, held, below, above, mine, arrived, moved, samples, sums, sems):
+def arrivals_kernel(
+    parts, held, velocity_below, velocity_above, position_below, position_above, mine, arrived, moved, samples, sums, place, sems
+):
     del held
-    copies = [
-        pltpu.make_async_copy(below, moved.at[:, 0, 0:MOVE], sems.at[0]),
-        pltpu.make_async_copy(above, moved.at[:, 0, MOVE + CAP : OUTCAP], sems.at[1]),
-        pltpu.make_async_copy(sums, samples, sems.at[2]),
-    ]
-    copies[0].start()
-    copies[1].start()
+    copies = []
+    ends = ((0, position_below, velocity_below), (MOVE + CAP, position_above, velocity_above))
+    for i, (at, position, velocity) in enumerate(ends):
+        copies.append(pltpu.make_async_copy(velocity, moved.at[3:6, 0, at : at + MOVE], sems.at[2 * i]))
+        copies[-1].start()
+    for i, (at, position, velocity) in enumerate(ends):
+        for c in range(3):
+            place[i, c] = position[c] + time_step * velocity[c]
+        copies.append(pltpu.make_async_copy(place.at[i], moved.at[0:3, 0, at : at + MOVE], sems.at[2 * i + 1]))
+        copies[-1].start()
     sums[:, 0] = (mine[...] + arrived[...]) * (1.0 / (PART * parts))
-    copies[2].start()
+    copies.append(pltpu.make_async_copy(sums, samples, sems.at[4]))
+    copies[-1].start()
     for c in copies:
         c.wait()
 
@@ -287,14 +296,15 @@
     f32 = jnp.float32
     limit = pltpu.CompilerParams(vmem_limit_bytes=32 * 2**20)
 
-    sent = jax.ShapeDtypeStruct((6, MOVE, PART), f32)
-    up, down, *held = pl.pallas_call(
-        movers_kernel,
+    sent = jax.ShapeDtypeStruct((3, MOVE, PART), f32)
+    up_position, down_position, selected, targets, orders, takens, turns, data, cells = pl.pallas_call(
+        position_kernel,
         in_specs=[HBM] * 6,
-        out_specs=[VMEM] * 8,
+        out_specs=[VMEM] * 9,
         out_shape=[
             sent,
             sent,
+            pltpu.VMEM((2 * MOVE, CAP), jnp.bfloat16),
             pltpu.VMEM((1, CAP), jnp.int32),
             pltpu.VMEM((1, CAP, PART), jnp.int32),
             pltpu.VMEM((1, PAIRS, CAP), jnp.int32),
@@ -305,28 +315,38 @@
         scratch_shapes=[pltpu.SemaphoreType.DMA((7,))],
         compiler_params=limit,
     )(*in_hbm(destination, pair_order, accepted, direction, particles, cell_index))
-    from_lower = from_behind(up, "space", 1)
-    from_upper = from_behind(down, "space", -1)
+    position_below = from_behind(up_position, "space", 1)
+    position_above = from_behind(down_position, "space", -1)
+    up_velocity, down_velocity = pl.pallas_call(
+        velocity_kernel,
+        in_specs=[VMEM] * 5,
+        out_specs=[VMEM] * 2,
+        out_shape=[sent, sent],
+        compiler_params=limit,
+    )(selected, orders, takens, turns, data)
+    velocity_below = from_behind(up_velocity, "space", 1)
+    velocity_above = from_behind(down_velocity, "space", -1)
+    held = (targets, orders, takens, turns, data, cells)
 
     half = jax.ShapeDtypeStruct((4, CELLS // 2), f32)
     moved, mine, theirs = pl.pallas_call(
         own_kernel,
-        in_specs=[SMEM] + [VMEM] * 6,
+        in_specs=[SMEM] + [VMEM] * 6 + [HBM],
         out_specs=[HBM, VMEM, VMEM],
         out_shape=[jax.ShapeDtypeStruct((6, 1, OUTCAP, PART), f32), half, half],
         scratch_shapes=[pltpu.VMEM((6, CAP, PART), f32), pltpu.SemaphoreType.DMA((CAP // PART,))],
         compiler_params=limit,
-    )(live_count, *held)
+    )(live_count, *held, down_velocity)
     arrived = from_behind(theirs, "rep", 1)
     moved, samples = pl.pallas_call(
         functools.partial(arrivals_kernel, parts),
-        in_specs=[HBM, VMEM, VMEM, VMEM, VMEM],
+        in_specs=[HBM] + [VMEM] * 6,
         out_specs=[HBM, HBM],
         out_shape=[jax.ShapeDtypeStruct(moved.shape, f32), jax.ShapeDtypeStruct((4, 1, CELLS // 2), f32)],
         input_output_aliases={0: 0},
-        scratch_shapes=[pltpu.VMEM((4, 1, CELLS // 2), f32), pltpu.SemaphoreType.DMA((3,))],
+        scratch_shapes=[pltpu.VMEM((4, 1, CELLS // 2), f32), pltpu.VMEM((2, 3, MOVE, PART), f32), pltpu.SemaphoreType.DMA((5,))],
         compiler_params=pltpu.CompilerParams(vmem_limit_bytes=8 * 2**20),
-    )(moved, from_lower, from_upper, mine, arrived)
+    )(moved, velocity_below, velocity_above, position_below, position_above, mine, arrived)
     return (moved, samples)
 
 

time: 23 us -> 27 us (1.17)
  starting transfers between devices: 10.4 us -> 17.9 us
  waiting for transfers between devices: 4.25 us -> 0.83 us
    ppermute x3 -> x5, starting transfers between devices: 10.4 us -> 17.9 us  [from_behind(): return lax.ppermute(value, axis, pairs)]
    ppermute x3 -> x5, waiting for transfers between devices: 4.25 us -> 0.83 us  [from_behind(): return lax.ppermute(value, axis, pairs)]
    pallas_call x3 -> x4, Pallas kernels: 6.86 us -> 6.73 us  [the longest x1 2.82 us: per_device(): pl.pallas_call(own_kernel, in_specs=[SMEM] + [VMEM] * 6 + [HBM], out_spec...]
  transfers between devices with their start and end apart: 3 -> 5, of which waited for: 2 -> 1; matrix products, arithmetic and copies ran while one was open for 0% -> 0% of each run, Pallas kernels for 12% -> 15%
where the time goes in v6:
time: 27 us; the launch traced here: 26.8 us
  starting transfers between devices  17.9 us (66%)
  Pallas kernels  6.73 us (25%)
  between operations  1.33 us (5%)
  waiting for transfers between devices  0.83 us (3%)
    ppermute x5, starting transfers between devices, from_behind(): return lax.ppermute(value, axis, pairs)  17.9 us
    pallas_call x1, Pallas kernels, per_device(): pl.pallas_call(own_kernel, in_specs=[SMEM] + [VMEM] * 6 + [HBM], out_spec...  2.82 us
    pallas_call x1, Pallas kernels, per_device(): pl.pallas_call(position_kernel, in_specs=[HBM] * 6, out_specs=[VMEM] * 9,...  1.82 us
    pallas_call x1, Pallas kernels, per_device(): pl.pallas_call(velocity_kernel, in_specs=[VMEM] * 5, out_specs=[VMEM] * 2...  1.16 us
    pallas_call x1, Pallas kernels, per_device(): pl.pallas_call(functools.partial(arrivals_kernel, parts), in_specs=[HBM]...  0.92 us
    ppermute x5, waiting for transfers between devices, from_behind(): return lax.ppermute(value, axis, pairs)  0.83 us
  transfers between devices with their start and end apart: 5, of which 1 were waited for; matrix products, arithmetic and copies ran while one was open for 0% of the time, Pallas kernels for 15%

profile of v6, /device:TPU:1, one launch (start us, length us, event | category | flops | bytes accessed | tf_op | source)
XLA Modules:
  0.0 26.8 jit_solution(8483491888094096086)
XLA Ops:
  0.6 1.8 %shard_map.86 = (f32[3,128,128]{2,1,0:T(8,128)S(1)}, f32[3,128,128]{2,1,0:T(8,128)S(1)}, bf16[256,512]{1,0:T(8,128)(2,1)S(1)}, s32[1,512]{1,0:T(1,128)S(1)}, s32...) custom-call(s32[1,512]{1,0:T(1,128)} %destination.1, ...), custom_call_target="tpu_custom_call" | custom-call | tf_op jit(solution)/shard_map/pallas_call | solution.py:300
  2.5 2.1 %collective-permute-start.2 = (f32[3,128,128]{2,1,0:T(8,128)S(1)}, f32[3,128,128]{2,1,0:T(8,128)S(1)}, u32[]{:S(2)}, u32[]{:S(2)}) collective-permute-start(f32[3,128,128]{2,1,0:T(8,128)S(1)} %get-tuple-element.26), channel_id=1, source_target_pairs={{0,1},{1,2},{2,3},{3,4},{4,5},{5,6},{6,7},{7,8},{8,9},{9,10},{10,1... | collective-permute-start | bytes 589832 | tf_op jit(solution)/shard_map/ppermute | solution.py:289
  4.6 7.3 %collective-permute-start.3 = (f32[3,128,128]{2,1,0:T(8,128)S(1)}, f32[3,128,128]{2,1,0:T(8,128)S(1)}, u32[]{:S(2)}, u32[]{:S(2)}) collective-permute-start(f32[3,128,128]{2,1,0:T(8,128)S(1)} %get-tuple-element.27), channel_id=1, source_target_pairs={{0,63},{1,0},{2,1},{3,2},{4,3},{5,4},{6,5},{7,6},{8,7},{9,8},{10,9... | collective-permute-start | bytes 589832 | tf_op jit(solution)/shard_map/ppermute | solution.py:289
  11.8 1.2 %shard_map.87 = (f32[3,128,128]{2,1,0:T(8,128)S(1)}, f32[3,128,128]{2,1,0:T(8,128)S(1)}) custom-call(bf16[256,512]{1,0:T(8,128)(2,1)S(1)} %get-tuple-element.22.selected, s32[1,512,128]{2,1,0:T(8,128)S(1)} %get-tuple-element.17.orders.order, s32[1,64,512]{2,1,0:T(8,128)S(1)} %get-tuple-element.18.takens.accepted, ...), custom_call_target="tpu_custom_call" | custom-call | tf_op jit(solution)/shard_map/pallas_call | solution.py:320
  13.0 0.1 collective-permute-start
  13.1 6.9 %collective-permute-start.1 = (f32[3,128,128]{2,1,0:T(8,128)S(1)}, f32[3,128,128]{2,1,0:T(8,128)S(1)}, u32[]{:S(2)}, u32[]{:S(2)}) collective-permute-start(f32[3,128,128]{2,1,0:T(8,128)S(1)} %get-tuple-element.23.sent), channel_id=1, source_target_pairs={{0,63},{1,0},{2,1},{3,2},{4,3},{5,4},{6,5},{7,6},{8,7},{9,8},{10,9... | collective-permute-start | bytes 589832 | tf_op jit(solution)/shard_map/ppermute | solution.py:289
  20.6 2.8 %shard_map.88 = (f32[6,1,768,128]{3,2,1,0:T(8,128)}, f32[4,128]{1,0:T(4,128)S(1)}, f32[4,128]{1,0:T(4,128)S(1)}) custom-call(s32[1,1]{1,0:T(1,128)S(6)} %copy.11.live_count, s32[1,512]{1,0:T(1,128)S(1)} %get-tuple-element.16.destination, s32[1,512,128]{2,1,0:T(8,128)S(1)} %get-tuple-element.17.orders.order, ...), custom_call_target="tpu_custom_call" | custom-call | tf_op jit(solution)/shard_map/pallas_call | solution.py:332
  23.5 1.6 %collective-permute-start.4 = (f32[4,128]{1,0:T(4,128)S(1)}, f32[4,128]{1,0:T(4,128)S(1)}, u32[]{:S(2)}, u32[]{:S(2)}) collective-permute-start(f32[4,128]{1,0:T(4,128)S(1)} %get-tuple-element.29), channel_id=1, source_target_pairs={{0,64},{64,0},{1,65},{65,1},{2,66},{66,2},{3,67},{67,3},{4,68},{68... | collective-permute-start | bytes 6152 | tf_op jit(solution)/shard_map/ppermute | solution.py:289
  25.0 0.8 %collective-permute-done.4.arrived = f32[4,128]{1,0:T(4,128)S(1)} collective-permute-done((f32[4,128]{1,0:T(4,128)S(1)}, f32[4,128]{1,0:T(4,128)S(1)}, u32[]{:S(2)}, u32[]{:S(2)}) %collective-permute-start.4) | collective-permute-done | bytes 2080 | tf_op jit(solution)/shard_map/ppermute | solution.py:289
  25.9 0.0 collective-permute-done.2.position_below
  25.9 0.0 collective-permute-done.3.position_above
  25.9 0.0 collective-permute-done.velocity_below
  25.9 0.0 collective-permute-done.1.velocity_above
  25.9 0.9 %shard_map.89 = (f32[6,1,768,128]{3,2,1,0:T(8,128)}, f32[4,1,128]{2,1,0:T(1,128)}) custom-call(f32[6,1,768,128]{3,2,1,0:T(8,128)} %get-tuple-element.24.held, f32[3,128,128]{2,1,0:T(8,128)S(1)} %collective-permute-done.velocity_below, f32[3,128,128]{2,1,0:T(8,128)S(1)} %collective-permute-done.1.velocity_above, ...), custom_call_target="tpu_custom_call", output_to_operand_aliasing={{0}: (0, {})} | custom-call | tf_op jit(solution)/shard_map/pallas_call | solution.py:341
Async XLA Ops:
  2.5 23.4 %collective-permute-start.2 = (f32[3,128,128]{2,1,0:T(8,128)S(1)}, f32[3,128,128]{2,1,0:T(8,128)S(1)}, u32[]{:S(2)}, u32[]{:S(2)}) collective-permute-start(f32[3,128,128]{2,1,0:T(8,128)S(1)} %get-tuple-element.26), channel_id=1, source_target_pairs={{0,1},{1,2},{2,3},{3,4},{4,5},{5,6},{6,7},{7,8},{8,9},{9,10},{10,1... | collective-permute-start | bytes 589832 | tf_op jit(solution)/shard_map/ppermute | solution.py:289
  4.6 21.3 %collective-permute-start.3 = (f32[3,128,128]{2,1,0:T(8,128)S(1)}, f32[3,128,128]{2,1,0:T(8,128)S(1)}, u32[]{:S(2)}, u32[]{:S(2)}) collective-permute-start(f32[3,128,128]{2,1,0:T(8,128)S(1)} %get-tuple-element.27), channel_id=1, source_target_pairs={{0,63},{1,0},{2,1},{3,2},{4,3},{5,4},{6,5},{7,6},{8,7},{9,8},{10,9... | collective-permute-start | bytes 589832 | tf_op jit(solution)/shard_map/ppermute | solution.py:289
  13.0 12.9 %collective-permute-start = (f32[3,128,128]{2,1,0:T(8,128)S(1)}, f32[3,128,128]{2,1,0:T(8,128)S(1)}, u32[]{:S(2)}, u32[]{:S(2)}) collective-permute-start(f32[3,128,128]{2,1,0:T(8,128)S(1)} %get-tuple-element.25), channel_id=1, source_target_pairs={{0,1},{1,2},{2,3},{3,4},{4,5},{5,6},{6,7},{7,8},{8,9},{9,10},{10,1... | collective-permute-start | bytes 589832 | tf_op jit(solution)/shard_map/ppermute | solution.py:289
  13.1 12.8 %collective-permute-start.1 = (f32[3,128,128]{2,1,0:T(8,128)S(1)}, f32[3,128,128]{2,1,0:T(8,128)S(1)}, u32[]{:S(2)}, u32[]{:S(2)}) collective-permute-start(f32[3,128,128]{2,1,0:T(8,128)S(1)} %get-tuple-element.23.sent), channel_id=1, source_target_pairs={{0,63},{1,0},{2,1},{3,2},{4,3},{5,4},{6,5},{7,6},{8,7},{9,8},{10,9... | collective-permute-start | bytes 589832 | tf_op jit(solution)/shard_map/ppermute | solution.py:289
  23.5 2.4 %collective-permute-start.4 = (f32[4,128]{1,0:T(4,128)S(1)}, f32[4,128]{1,0:T(4,128)S(1)}, u32[]{:S(2)}, u32[]{:S(2)}) collective-permute-start(f32[4,128]{1,0:T(4,128)S(1)} %get-tuple-element.29), channel_id=1, source_target_pairs={{0,64},{64,0},{1,65},{65,1},{2,66},{66,2},{3,67},{67,3},{4,68},{68... | collective-permute-start | bytes 6152 | tf_op jit(solution)/shard_map/ppermute | solution.py:289

commit v7 on v5

--- a/solution.py
+++ b/solution.py
@@ -56,12 +56,7 @@
 
 
 def swap_sublanes(x, distance):
-    if distance == 4:
-        return pltpu.roll(x, 4, 1)
-    ahead = pltpu.roll(x, 8 - distance, 1)
-    behind = pltpu.roll(x, distance, 1)
-    low = (lax.broadcasted_iota(jnp.int32, x.shape, 1) & distance) == 0
-    return jnp.where(low, ahead, behind)
+    return jnp.take_along_axis(x, lax.broadcasted_iota(jnp.int32, x.shape, 0) ^ distance, axis=0)
 
 
 def sort_rows(keys):
@@ -84,7 +79,7 @@
         low = (sub & distance) == 0
         new = []
         for x in rows:
-            y = swap_sublanes(x[None], distance)[0]
+            y = swap_sublanes(x, distance)
             new.append(jnp.where(low, jnp.minimum(x, y), jnp.maximum(x, y)))
         return new
 
@@ -139,19 +134,30 @@
 
 
 def pick(selection, x):
-    high, low = split(x)
-    return dot(selection, high) + dot(selection, low)
+    both = dot(selection, jnp.concatenate(split(x), axis=1))
+    return both[:, :PART] + both[:, PART:]
 
 
 def mover_selection(destination):
     up = destination == neighbour(1)
     down = destination == neighbour(-1)
-    ahead = lax.broadcasted_iota(jnp.int32, (CAP, CAP), 0) < lax.broadcasted_iota(jnp.int32, (CAP, CAP), 1)
-    flags = jnp.concatenate([jnp.where(up, 1.0, 0.0), jnp.where(down, 1.0, 0.0), jnp.zeros((6, CAP), jnp.float32)], axis=0)
-    ranking = dot(flags.astype(jnp.bfloat16), jnp.where(ahead, 1.0, 0.0).astype(jnp.bfloat16))
-    rows = lax.broadcasted_iota(jnp.int32, (MOVE, CAP), 0).astype(jnp.float32)
-    chosen = [rows == jnp.where(moving, ranking[i : i + 1], -1.0) for i, moving in enumerate((up, down))]
-    return jnp.where(jnp.concatenate(chosen, axis=0), 1.0, 0.0).astype(jnp.bfloat16)
+    pieces = CAP // PART
+    flags = jnp.concatenate(
+        [jnp.where(m[:, i * PART : (i + 1) * PART], 1.0, 0.0) for m in (up, down) for i in range(pieces)], axis=0
+    )
+    ahead = lax.broadcasted_iota(jnp.int32, (PART, 2 * PART), 0) < lax.broadcasted_iota(jnp.int32, (PART, 2 * PART), 1)
+    counts = dot(flags.astype(jnp.bfloat16), jnp.where(ahead, 1.0, 0.0).astype(jnp.bfloat16))
+    rows = lax.broadcasted_iota(jnp.int32, (MOVE, PART), 0).astype(jnp.float32)
+    chosen = []
+    for d in range(2):
+        parts, before = [], jnp.zeros((1, PART), jnp.float32)
+        for i in range(pieces):
+            at = pieces * d + i
+            ranking = jnp.where(flags[at : at + 1] > 0.5, counts[at : at + 1, :PART] + before, -1.0)
+            before += counts[at : at + 1, PART:]
+            parts.append(jnp.where(rows == ranking, 1.0, 0.0).astype(jnp.bfloat16))
+        chosen.append(jnp.concatenate(parts, axis=1))
+    return jnp.concatenate(chosen, axis=0)
 
 
 def place_on_mesh():
@@ -171,10 +177,10 @@
         for i, (source, target) in enumerate(
             (
                 (destination, targets),
+                (particles.at[3:6], data.at[3:6]),
                 (order, orders),
                 (accepted, takens),
                 (direction, turns),
-                (particles.at[3:6], data.at[3:6]),
                 (particles.at[0:3], data.at[0:3]),
                 (cell, cells),
             )
@@ -184,26 +190,24 @@
         c.start()
     copies[0].wait()
     selection = mover_selection(targets[...])
-    for c in copies[1:4]:
+    copies[1].wait()
+    velocity = [pick(selection, data[3 + c, 0]) for c in range(3)]
+    for c in copies[2:]:
         c.wait()
     info = jnp.where(takens[0] == 1, turns[0], -1).astype(jnp.float32).astype(jnp.bfloat16)
     chosen = dot_lanes(info, selection)
     order_rows = dot(selection, orders[0].astype(jnp.float32).astype(jnp.bfloat16))
+    position = [pick(selection, data[c, 0]) for c in range(3)]
     codes = []
     for i in range(2):
         part = slice(i * MOVE, (i + 1) * MOVE)
         codes.append(partner_codes(order_rows[part].T, chosen[:, part]).T.astype(jnp.int32))
-    copies[4].wait()
-    velocity = [pick(selection, data[3 + c, 0]) for c in range(3)]
-    copies[5].wait()
-    position = [pick(selection, data[c, 0]) for c in range(3)]
     for i, out in enumerate((up, down)):
         part = slice(i * MOVE, (i + 1) * MOVE)
         result = collide([v[part] for v in velocity], codes[i])
         for c in range(3):
             out[3 + c] = result[c]
             out[c] = position[c][part] + time_step * result[c]
-    copies[6].wait()
 
 
 def own_kernel(live_count, destination, order, accepted, direction, particles, cells, moved, mine, theirs, out, sems):

time: 23 us -> 22.6 us (0.983)
  Pallas kernels: 6.86 us -> 6.4 us
    pallas_call x1, Pallas kernels: 3.13 us -> 2.77 us  [per_device(): pl.pallas_call(movers_kernel, in_specs=[HBM] * 6, out_specs=[VMEM] * 8, o...]
where the time goes in v7:
time: 22.6 us; the launch traced here: 22.5 us
  starting transfers between devices  10.4 us (46%)
  Pallas kernels  6.4 us (28%)
  waiting for transfers between devices  4.34 us (19%)
  between operations  1.3 us (6%)
    ppermute x3, starting transfers between devices, from_behind(): return lax.ppermute(value, axis, pairs)  10.4 us
    ppermute x3, waiting for transfers between devices, from_behind(): return lax.ppermute(value, axis, pairs)  4.34 us
    pallas_call x1, Pallas kernels, per_device(): pl.pallas_call(movers_kernel, in_specs=[HBM] * 6, out_specs=[VMEM] * 8, o...  2.77 us
    pallas_call x1, Pallas kernels, per_device(): pl.pallas_call(own_kernel, in_specs=[SMEM] + [VMEM] * 6, out_specs=[HBM,...  2.73 us
    pallas_call x1, Pallas kernels, per_device(): pl.pallas_call(functools.partial(arrivals_kernel, parts), in_specs=[HBM,...  0.9 us
  transfers between devices with their start and end apart: 3, of which 2 were waited for; matrix products, arithmetic and copies ran while one was open for 0% of the time, Pallas kernels for 12%

profile of v7, /device:TPU:1, one launch (start us, length us, event | category | flops | bytes accessed | tf_op | source)
XLA Modules:
  0.0 22.5 jit_solution(12788248350276928234)
XLA Ops:
  0.6 2.8 %shard_map.86 = (f32[6,128,128]{2,1,0:T(8,128)S(1)}, f32[6,128,128]{2,1,0:T(8,128)S(1)}, s32[1,512]{1,0:T(1,128)S(1)}, s32[1,512,128]{2,1,0:T(8,128)S(1)}, s32[1...) custom-call(s32[1,512]{1,0:T(1,128)} %destination.1, ...), custom_call_target="tpu_custom_call" | custom-call | tf_op jit(solution)/shard_map/pallas_call | solution.py:295
  3.4 2.1 %collective-permute-start = (f32[6,128,128]{2,1,0:T(8,128)S(1)}, f32[6,128,128]{2,1,0:T(8,128)S(1)}, u32[]{:S(2)}, u32[]{:S(2)}) collective-permute-start(f32[6,128,128]{2,1,0:T(8,128)S(1)} %get-tuple-element.20), channel_id=1, source_target_pairs={{0,1},{1,2},{2,3},{3,4},{4,5},{5,6},{6,7},{7,8},{8,9},{9,10},{10,1... | collective-permute-start | bytes 1179656 | tf_op jit(solution)/shard_map/ppermute | solution.py:284
  5.5 7.3 %collective-permute-start.1 = (f32[6,128,128]{2,1,0:T(8,128)S(1)}, f32[6,128,128]{2,1,0:T(8,128)S(1)}, u32[]{:S(2)}, u32[]{:S(2)}) collective-permute-start(f32[6,128,128]{2,1,0:T(8,128)S(1)} %get-tuple-element.21), channel_id=1, source_target_pairs={{0,63},{1,0},{2,1},{3,2},{4,3},{5,4},{6,5},{7,6},{8,7},{9,8},{10,9... | collective-permute-start | bytes 1179656 | tf_op jit(solution)/shard_map/ppermute | solution.py:284
  13.4 2.7 %shard_map.87 = (f32[6,1,768,128]{3,2,1,0:T(8,128)}, f32[4,128]{1,0:T(4,128)S(1)}, f32[4,128]{1,0:T(4,128)S(1)}) custom-call(s32[1,1]{1,0:T(1,128)S(6)} %copy.11.live_count, s32[1,512]{1,0:T(1,128)S(1)} %get-tuple-element.13.destination, s32[1,512,128]{2,1,0:T(8,128)S(1)} %get-tuple-element.14.order, s32[1,64,512]{2,1,0:T(8,128)S(1)} %get-tuple-element.15.accepted, ...), custom_call_target="tpu_custom_call" | custom-call | tf_op jit(solution)/shard_map/pallas_call | solution.py:316
  16.2 1.0 %collective-permute-start.2 = (f32[4,128]{1,0:T(4,128)S(1)}, f32[4,128]{1,0:T(4,128)S(1)}, u32[]{:S(2)}, u32[]{:S(2)}) collective-permute-start(f32[4,128]{1,0:T(4,128)S(1)} %get-tuple-element.23), channel_id=1, source_target_pairs={{0,64},{64,0},{1,65},{65,1},{2,66},{66,2},{3,67},{67,3},{4,68},{68... | collective-permute-start | bytes 6152 | tf_op jit(solution)/shard_map/ppermute | solution.py:284
  17.2 0.8 %collective-permute-done.2.arrived = f32[4,128]{1,0:T(4,128)S(1)} collective-permute-done((f32[4,128]{1,0:T(4,128)S(1)}, f32[4,128]{1,0:T(4,128)S(1)}, u32[]{:S(2)}, u32[]{:S(2)}) %collective-permute-start.2) | collective-permute-done | bytes 2080 | tf_op jit(solution)/shard_map/ppermute | solution.py:284
  18.0 3.5 %collective-permute-done.below = f32[6,128,128]{2,1,0:T(8,128)S(1)} collective-permute-done((f32[6,128,128]{2,1,0:T(8,128)S(1)}, f32[6,128,128]{2,1,0:T(8,128)S(1)}, u32[]{:S(2)}, u32[]{:S(2)}) %collective-permute-start) | collective-permute-done | bytes 393248 | tf_op jit(solution)/shard_map/ppermute | solution.py:284
  21.5 0.0 collective-permute-done.1.above
  21.5 0.9 %shard_map.88 = (f32[6,1,768,128]{3,2,1,0:T(8,128)}, f32[4,1,128]{2,1,0:T(1,128)}) custom-call(f32[6,1,768,128]{3,2,1,0:T(8,128)} %get-tuple-element.19.held, f32[6,128,128]{2,1,0:T(8,128)S(1)} %collective-permute-done.below, f32[6,128,128]{2,1,0:T(8,128)S(1)} %collective-permute-done.1.above, ...), custom_call_target="tpu_custom_call", output_to_operand_aliasing={{0}: (0, {})} | custom-call | tf_op jit(solution)/shard_map/pallas_call | solution.py:325
Async XLA Ops:
  3.4 18.1 %collective-permute-start = (f32[6,128,128]{2,1,0:T(8,128)S(1)}, f32[6,128,128]{2,1,0:T(8,128)S(1)}, u32[]{:S(2)}, u32[]{:S(2)}) collective-permute-start(f32[6,128,128]{2,1,0:T(8,128)S(1)} %get-tuple-element.20), channel_id=1, source_target_pairs={{0,1},{1,2},{2,3},{3,4},{4,5},{5,6},{6,7},{7,8},{8,9},{9,10},{10,1... | collective-permute-start | bytes 1179656 | tf_op jit(solution)/shard_map/ppermute | solution.py:284
  5.5 16.0 %collective-permute-start.1 = (f32[6,128,128]{2,1,0:T(8,128)S(1)}, f32[6,128,128]{2,1,0:T(8,128)S(1)}, u32[]{:S(2)}, u32[]{:S(2)}) collective-permute-start(f32[6,128,128]{2,1,0:T(8,128)S(1)} %get-tuple-element.21), channel_id=1, source_target_pairs={{0,63},{1,0},{2,1},{3,2},{4,3},{5,4},{6,5},{7,6},{8,7},{9,8},{10,9... | collective-permute-start | bytes 1179656 | tf_op jit(solution)/shard_map/ppermute | solution.py:284
  16.2 1.9 %collective-permute-start.2 = (f32[4,128]{1,0:T(4,128)S(1)}, f32[4,128]{1,0:T(4,128)S(1)}, u32[]{:S(2)}, u32[]{:S(2)}) collective-permute-start(f32[4,128]{1,0:T(4,128)S(1)} %get-tuple-element.23), channel_id=1, source_target_pairs={{0,64},{64,0},{1,65},{65,1},{2,66},{66,2},{3,67},{67,3},{4,68},{68... | collective-permute-start | bytes 6152 | tf_op jit(solution)/shard_map/ppermute | solution.py:284

commit v8 on v7

--- a/solution.py
+++ b/solution.py
@@ -177,11 +177,10 @@
         for i, (source, target) in enumerate(
             (
                 (destination, targets),
-                (particles.at[3:6], data.at[3:6]),
                 (order, orders),
                 (accepted, takens),
                 (direction, turns),
-                (particles.at[0:3], data.at[0:3]),
+                (particles, data),
                 (cell, cells),
             )
         )
@@ -190,24 +189,25 @@
         c.start()
     copies[0].wait()
     selection = mover_selection(targets[...])
-    copies[1].wait()
-    velocity = [pick(selection, data[3 + c, 0]) for c in range(3)]
-    for c in copies[2:]:
+    for c in copies[1:4]:
         c.wait()
     info = jnp.where(takens[0] == 1, turns[0], -1).astype(jnp.float32).astype(jnp.bfloat16)
-    chosen = dot_lanes(info, selection)
-    order_rows = dot(selection, orders[0].astype(jnp.float32).astype(jnp.bfloat16))
-    position = [pick(selection, data[c, 0]) for c in range(3)]
+    flipped = orders[0].astype(jnp.float32).T.astype(jnp.bfloat16)
+    picked = dot_lanes(jnp.concatenate([flipped, info], axis=0), selection)
     codes = []
     for i in range(2):
         part = slice(i * MOVE, (i + 1) * MOVE)
-        codes.append(partner_codes(order_rows[part].T, chosen[:, part]).T.astype(jnp.int32))
+        codes.append(partner_codes(picked[:PART, part], picked[PART:, part]).T.astype(jnp.int32))
+    copies[4].wait()
+    velocity = [pick(selection, data[3 + c, 0]) for c in range(3)]
+    position = [pick(selection, data[c, 0]) for c in range(3)]
     for i, out in enumerate((up, down)):
         part = slice(i * MOVE, (i + 1) * MOVE)
         result = collide([v[part] for v in velocity], codes[i])
         for c in range(3):
             out[3 + c] = result[c]
             out[c] = position[c][part] + time_step * result[c]
+    copies[5].wait()
 
 
 def own_kernel(live_count, destination, order, accepted, direction, particles, cells, moved, mine, theirs, out, sems):
@@ -306,7 +306,7 @@
             pltpu.VMEM((6, 1, CAP, PART), f32),
             pltpu.VMEM((1, CAP), jnp.int32),
         ],
-        scratch_shapes=[pltpu.SemaphoreType.DMA((7,))],
+        scratch_shapes=[pltpu.SemaphoreType.DMA((6,))],
         compiler_params=limit,
     )(*in_hbm(destination, pair_order, accepted, direction, particles, cell_index))
     from_lower = from_behind(up, "space", 1)

time: 22.6 us -> 22.3 us (0.987)
  Pallas kernels: 6.4 us -> 6.15 us
    pallas_call x1, Pallas kernels: 2.77 us -> 2.51 us  [per_device(): pl.pallas_call(movers_kernel, in_specs=[HBM] * 6, out_specs=[VMEM] * 8, o...]
where the time goes in v8:
time: 22.3 us; the launch traced here: 22.2 us
  starting transfers between devices  10.4 us (47%)
  Pallas kernels  6.15 us (28%)
  waiting for transfers between devices  4.32 us (19%)
  between operations  1.3 us (6%)
    ppermute x3, starting transfers between devices, from_behind(): return lax.ppermute(value, axis, pairs)  10.4 us
    ppermute x3, waiting for transfers between devices, from_behind(): return lax.ppermute(value, axis, pairs)  4.32 us
    pallas_call x1, Pallas kernels, per_device(): pl.pallas_call(own_kernel, in_specs=[SMEM] + [VMEM] * 6, out_specs=[HBM,...  2.73 us
    pallas_call x1, Pallas kernels, per_device(): pl.pallas_call(movers_kernel, in_specs=[HBM] * 6, out_specs=[VMEM] * 8, o...  2.51 us
    pallas_call x1, Pallas kernels, per_device(): pl.pallas_call(functools.partial(arrivals_kernel, parts), in_specs=[HBM,...  0.9 us
  transfers between devices with their start and end apart: 3, of which 2 were waited for; matrix products, arithmetic and copies ran while one was open for 0% of the time, Pallas kernels for 12%

profile of v8, /device:TPU:1, one launch (start us, length us, event | category | flops | bytes accessed | tf_op | source)
XLA Modules:
  0.0 22.2 jit_solution(8926047794265982455)
XLA Ops:
  0.6 2.5 %shard_map.86 = (f32[6,128,128]{2,1,0:T(8,128)S(1)}, f32[6,128,128]{2,1,0:T(8,128)S(1)}, s32[1,512]{1,0:T(1,128)S(1)}, s32[1,512,128]{2,1,0:T(8,128)S(1)}, s32[1...) custom-call(s32[1,512]{1,0:T(1,128)} %destination.1, ...), custom_call_target="tpu_custom_call" | custom-call | tf_op jit(solution)/shard_map/pallas_call | solution.py:295
  3.2 2.1 %collective-permute-start = (f32[6,128,128]{2,1,0:T(8,128)S(1)}, f32[6,128,128]{2,1,0:T(8,128)S(1)}, u32[]{:S(2)}, u32[]{:S(2)}) collective-permute-start(f32[6,128,128]{2,1,0:T(8,128)S(1)} %get-tuple-element.20), channel_id=1, source_target_pairs={{0,1},{1,2},{2,3},{3,4},{4,5},{5,6},{6,7},{7,8},{8,9},{9,10},{10,1... | collective-permute-start | bytes 1179656 | tf_op jit(solution)/shard_map/ppermute | solution.py:284
  5.3 7.3 %collective-permute-start.1 = (f32[6,128,128]{2,1,0:T(8,128)S(1)}, f32[6,128,128]{2,1,0:T(8,128)S(1)}, u32[]{:S(2)}, u32[]{:S(2)}) collective-permute-start(f32[6,128,128]{2,1,0:T(8,128)S(1)} %get-tuple-element.21), channel_id=1, source_target_pairs={{0,63},{1,0},{2,1},{3,2},{4,3},{5,4},{6,5},{7,6},{8,7},{9,8},{10,9... | collective-permute-start | bytes 1179656 | tf_op jit(solution)/shard_map/ppermute | solution.py:284
  13.2 2.7 %shard_map.87 = (f32[6,1,768,128]{3,2,1,0:T(8,128)}, f32[4,128]{1,0:T(4,128)S(1)}, f32[4,128]{1,0:T(4,128)S(1)}) custom-call(s32[1,1]{1,0:T(1,128)S(6)} %copy.11.live_count, s32[1,512]{1,0:T(1,128)S(1)} %get-tuple-element.13.destination, s32[1,512,128]{2,1,0:T(8,128)S(1)} %get-tuple-element.14.order, s32[1,64,512]{2,1,0:T(8,128)S(1)} %get-tuple-element.15.accepted, ...), custom_call_target="tpu_custom_call" | custom-call | tf_op jit(solution)/shard_map/pallas_call | solution.py:316
  15.9 1.0 %collective-permute-start.2 = (f32[4,128]{1,0:T(4,128)S(1)}, f32[4,128]{1,0:T(4,128)S(1)}, u32[]{:S(2)}, u32[]{:S(2)}) collective-permute-start(f32[4,128]{1,0:T(4,128)S(1)} %get-tuple-element.23), channel_id=1, source_target_pairs={{0,64},{64,0},{1,65},{65,1},{2,66},{66,2},{3,67},{67,3},{4,68},{68... | collective-permute-start | bytes 6152 | tf_op jit(solution)/shard_map/ppermute | solution.py:284
  17.0 0.8 %collective-permute-done.2.arrived = f32[4,128]{1,0:T(4,128)S(1)} collective-permute-done((f32[4,128]{1,0:T(4,128)S(1)}, f32[4,128]{1,0:T(4,128)S(1)}, u32[]{:S(2)}, u32[]{:S(2)}) %collective-permute-start.2) | collective-permute-done | bytes 2080 | tf_op jit(solution)/shard_map/ppermute | solution.py:284
  17.8 3.5 %collective-permute-done.below = f32[6,128,128]{2,1,0:T(8,128)S(1)} collective-permute-done((f32[6,128,128]{2,1,0:T(8,128)S(1)}, f32[6,128,128]{2,1,0:T(8,128)S(1)}, u32[]{:S(2)}, u32[]{:S(2)}) %collective-permute-start) | collective-permute-done | bytes 393248 | tf_op jit(solution)/shard_map/ppermute | solution.py:284
  21.3 0.0 collective-permute-done.1.above
  21.3 0.9 %shard_map.88 = (f32[6,1,768,128]{3,2,1,0:T(8,128)}, f32[4,1,128]{2,1,0:T(1,128)}) custom-call(f32[6,1,768,128]{3,2,1,0:T(8,128)} %get-tuple-element.19.held, f32[6,128,128]{2,1,0:T(8,128)S(1)} %collective-permute-done.below, f32[6,128,128]{2,1,0:T(8,128)S(1)} %collective-permute-done.1.above, ...), custom_call_target="tpu_custom_call", output_to_operand_aliasing={{0}: (0, {})} | custom-call | tf_op jit(solution)/shard_map/pallas_call | solution.py:325
Async XLA Ops:
  3.2 18.1 %collective-permute-start = (f32[6,128,128]{2,1,0:T(8,128)S(1)}, f32[6,128,128]{2,1,0:T(8,128)S(1)}, u32[]{:S(2)}, u32[]{:S(2)}) collective-permute-start(f32[6,128,128]{2,1,0:T(8,128)S(1)} %get-tuple-element.20), channel_id=1, source_target_pairs={{0,1},{1,2},{2,3},{3,4},{4,5},{5,6},{6,7},{7,8},{8,9},{9,10},{10,1... | collective-permute-start | bytes 1179656 | tf_op jit(solution)/shard_map/ppermute | solution.py:284
  5.3 16.0 %collective-permute-start.1 = (f32[6,128,128]{2,1,0:T(8,128)S(1)}, f32[6,128,128]{2,1,0:T(8,128)S(1)}, u32[]{:S(2)}, u32[]{:S(2)}) collective-permute-start(f32[6,128,128]{2,1,0:T(8,128)S(1)} %get-tuple-element.21), channel_id=1, source_target_pairs={{0,63},{1,0},{2,1},{3,2},{4,3},{5,4},{6,5},{7,6},{8,7},{9,8},{10,9... | collective-permute-start | bytes 1179656 | tf_op jit(solution)/shard_map/ppermute | solution.py:284
  15.9 1.9 %collective-permute-start.2 = (f32[4,128]{1,0:T(4,128)S(1)}, f32[4,128]{1,0:T(4,128)S(1)}, u32[]{:S(2)}, u32[]{:S(2)}) collective-permute-start(f32[4,128]{1,0:T(4,128)S(1)} %get-tuple-element.23), channel_id=1, source_target_pairs={{0,64},{64,0},{1,65},{65,1},{2,66},{66,2},{3,67},{67,3},{4,68},{68... | collective-permute-start | bytes 6152 | tf_op jit(solution)/shard_map/ppermute | solution.py:284
